TPU v7x, 256 devices: a whole 4x4x8 slice. The times are simulated.
256 devices in a mesh: rows: 64 (over y, z, core), rhs: 4 (over x).
Axes of the slice: x: 4, y: 4, z: 8, core: 2. Of those that a mesh axis runs over, the one named last changes fastest.
Arguments:
- right_side: bfloat16 [16, 64, 256, 128], P(None, 'rows', 'rhs'), may hold values from -6 to 6
- lower: bfloat16 [16, 64, 4, 128, 128], P(None, 'rows', 'rhs'), may hold values from -0.1875 to 0.1875
- diag_inv: bfloat16 [16, 64, 128, 128], P(None, 'rows'), may hold values from -0.5 to 0.5
- levels: int32 [16, 64], replicated, may hold values from 0 to 7, as said below
- columns: int32 [16, 64, 4], P(None, 'rows'), may hold values from -1 to 1023, as said below
Outputs:
- solved: bfloat16 [16, 64, 256, 128], P(None, 'rows', 'rhs')
Inputs may be any that keep to these rules, and one draw needn't show every extreme that they name: `levels`: every index of rows holds exactly 2 block rows of each level. `columns`: level 0 block rows hold only -1. A block row of level l > 0 holds no -1; its slot 0 names a block row of level l - 1, the other slots block rows of levels below l. The stored blocks of one index's block rows of one level name block rows of any one index of rows at most 1 times, and exactly 1 times for some index.
All inputs are finite; a program needn't handle non-finite values.
Results may differ from a plain program's by a relative error of at most 0.0085.
Values may be sent and summed in bfloat16 or wider, within the bound.
No kernel may reach another device: no remote copies, remote signals or barrier semaphores. Data moves between devices by JAX's collectives and lax.ppermute only.
A program may use at most 64 MiB of HBM per device.

v0:
```python
import functools

import jax
import jax.numpy as jnp
from jax import lax
from jax.experimental import pallas as pl
from jax.experimental.pallas import tpu as pltpu
from jax.sharding import Mesh
from jax.sharding import PartitionSpec as P

LEVELS = 8
EACH = 2
NNZ = 4
SLOTS = EACH * NNZ
Y, Z, C, X = 4, 8, 2, 4
ROWS = ("y", "z", "core")
HALF = Z // 2
LINE = HALF * C * EACH
EARLY = 2
FIRST = EARLY * EACH
LATE = (LEVELS - EARLY) * EACH
GROUP = 3
GROUPS = (LEVELS - EARLY) // GROUP
SHARE = -(-GROUP * EACH // X)
PLACES = HALF * C * Y * EACH
BASE = 32
ABSENT = 255
VMEM = pl.BlockSpec(memory_space=pltpu.VMEM)
SMEM = pl.BlockSpec(memory_space=pltpu.SMEM)
ANY = pl.BlockSpec(memory_space=pl.ANY)
PARAMS = pltpu.CompilerParams(vmem_limit_bytes=16 * 2**20)
shape = jax.ShapeDtypeStruct


def swap(x, mask):
    return lax.ppermute(x, ROWS, [(i, i ^ mask) for i in range(Y * Z * C)])


def swap_y(pieces):
    return pieces[:1] + [swap(pieces[e], e * Z * C) for e in range(1, Y)]


def line_exchange(x, after=None, beside=None):
    chip = jnp.concatenate([x, swap(x, 1)], 0)
    if after is not None:
        chip, after = lax.optimization_barrier((chip, after))
    line = []
    for k in range(HALF):
        pairs = [(i, i ^ ((HALF * (i % C) + k) << 1)) for i in range(Y * Z * C)]
        line.append(lax.ppermute(chip, ROWS, pairs))
    half = jnp.concatenate(line, 0)
    if beside is not None:
        half, beside = lax.optimization_barrier((half, beside(after) if after is not None else beside))
    return (half, swap(half, 1)), beside


def times_transposed(x, w):
    return lax.dot_general(x, w, (((1,), (1,)), ((), ())), preferred_element_type=jnp.float32)


def run_copies(pairs, sems):
    copies = [pltpu.make_async_copy(a, b, sems.at[i]) for i, (a, b) in enumerate(pairs)]
    for c in copies:
        c.start()
    for c in copies:
        c.wait()


def quarters_of(order, rows, outs, at=0):
    part = outs[0].shape[1]
    y = order[order.shape[0] - 2]
    for e in range(Y):
        outs[e][at : at + rows.shape[0]] = rows[:, pl.ds(pl.multiple_of((y ^ e) * part, part), part), :]


def start_kernel(order, rhs, tiles, inverse, fresh, late_rows, rhs_early, inverse_early, early, *refs):
    payloads, (buf, factors, sems) = refs[:GROUPS], refs[GROUPS:]
    x = order[order.shape[0] - 1]
    rows = GROUP * EACH
    pairs = [(rhs.at[order[m]], buf.at[m]) for m in range(EACH)]
    pairs += [(inverse.at[order[m]], factors.at[m]) for m in range(EACH)]
    pairs += [(rhs.at[order[EACH + m]], rhs_early.at[m]) for m in range(EACH)]
    pairs += [(inverse.at[order[EACH + m]], inverse_early.at[m]) for m in range(EACH)]
    pairs += [(rhs.at[order[FIRST + p]], late_rows.at[p]) for p in range(LATE)]
    pairs += [(tiles.at[order[EACH + p]], early.at[p]) for p in range(EACH)]
    for g, payload in enumerate(payloads):
        start = FIRST + g * rows
        pairs += [(tiles.at[order[start + p]], payload.at[p]) for p in range(rows)]
        for p in range(SHARE):
            pairs.append((inverse.at[order[start + jnp.minimum(SHARE * x + p, rows - 1)]], payload.at[rows + p]))
    run_copies(pairs, sems)
    for m in range(EACH):
        fresh[m] = times_transposed(buf[m], factors[m]).astype(fresh.dtype)


def quarter_kernel(order, rows, rhs, inverse, digits, rhs_early, inverse_early, *messages):
    rhs_early[...] = rhs[...]
    inverse_early[...] = inverse[...]
    quarters_of(order, rows, messages)
    for e in range(Y):
        messages[e][LATE] = digits[...]


def select_kernel(codes, half, other, *messages):
    kept = (half, other)
    for e in range(Y):
        for s in range(SLOTS):
            code = codes[e * SLOTS + s]
            for o in range(2):

                @pl.when(code // LINE == o)
                def _(e=e, s=s, o=o, code=code):
                    messages[e][s] = kept[o][code % LINE]


def early_kernel(codes, order, rhs, inverse, tiles, *refs):
    messages, out, outs = refs[:Y], refs[Y], refs[Y + 1 :]
    x = order[order.shape[0] - 1]
    for m in range(EACH):
        total = rhs[m].astype(jnp.float32)
        for j in range(NNZ):
            s = m * NNZ + j
            source = codes[Y * SLOTS + s]
            known = messages[0][s]
            for e in range(1, Y):
                known = jnp.where(source == e, messages[e][s], known)
            total = total - times_transposed(known, tiles[x ^ j, m])
        out[m] = times_transposed(total.astype(jnp.bfloat16), inverse[m]).astype(out.dtype)
    quarters_of(order, out, outs)


def split_kernel(order, half, other, *messages):
    quarters_of(order, half, messages)
    quarters_of(order, other, messages, LINE)


def late_kernel(level, codes, order, factor, *refs):
    n = order.shape[0] - 2
    last = level == LEVELS - 1
    n_lines = 2 * (level - 1)
    rhs, oldest, lines, refs = refs[:Y], refs[Y : 2 * Y], refs[2 * Y : 2 * Y + n_lines], refs[2 * Y + n_lines :]
    solved, refs = (refs[: level - EARLY], refs[level - EARLY :]) if last else ([], refs)
    outs, store = refs[:-1], refs[-1]
    for e, piece in enumerate(oldest):
        at = e * 2 * LINE
        store[at // PLACES, at % PLACES : at % PLACES + 2 * LINE] = piece[...]
    for i, piece in enumerate(lines):
        store[2 + i] = piece[...]
    y = order[n]
    for e in range(Y):
        for m in range(EACH):
            p = (level - EARLY) * EACH + m
            q = p % (GROUP * EACH)
            at = [codes[(e * LATE + p) * NNZ + j] for j in range(NNZ)]
            known = jnp.concatenate([store[k // PLACES, k % PLACES] for k in at], 1)
            tiles = jnp.concatenate([factor[(y ^ e) * X + j, q] for j in range(NNZ)], 1)
            total = rhs[e][p].astype(jnp.float32) - times_transposed(known, tiles)
            inverse = factor[(y ^ e) * X + q // SHARE, GROUP * EACH + q % SHARE]
            x = times_transposed(total.astype(jnp.bfloat16), inverse).astype(jnp.bfloat16)
            if last:
                outs[e][p] = x
            else:
                outs[0][e * EACH + m] = x
    for k, piece in enumerate(solved):
        for e in range(Y):
            outs[e][k * EACH : (k + 1) * EACH] = piece[e * EACH : (e + 1) * EACH]


def gather_kernel(order, *refs):
    early, pieces, out = refs[:EARLY], refs[EARLY : EARLY + Y], refs[-1]
    y = order[order.shape[0] - 2]
    part = pieces[0].shape[1]
    for k in range(EARLY):
        for m in range(EACH):
            out[order[k * EACH + m]] = early[k][m]
    for p in range(LATE):
        for e in range(Y):
            out[order[FIRST + p], pl.ds(pl.multiple_of((y ^ e) * part, part), part), :] = pieces[e][p]


def spots_of(levels):
    row = jnp.arange(levels.shape[0], dtype=jnp.int32)
    earlier = row[None, :] < row[:, None]
    same = levels[:, None, :] == levels[None, :, :]
    return levels * EACH + jnp.sum(jnp.where(same & earlier[:, :, None], 1, 0), 1)


def make_codes(spot, columns, me):
    n, count = spot.shape
    row = jnp.arange(n, dtype=jnp.int32)
    people = me ^ (jnp.arange(Y, dtype=jnp.int32) * (Z * C))
    theirs = jnp.sum(
        jnp.where(people[:, None, None] == jnp.arange(count, dtype=jnp.int32)[None, None, :], spot[None], 0), 2
    )
    hit = theirs[:, None, :] == row[None, :, None]
    wanted = jnp.sum(jnp.where(hit[:, :, :, None], columns[:, None], 0), 2)
    wanted = wanted.reshape(-1)
    everyone = jnp.arange(spot.size, dtype=jnp.int32)
    found = jnp.sum(jnp.where(wanted[:, None] == everyone[None, :], spot.reshape(-1)[None, :], 0), 1)
    apart = (wanted % count) ^ me
    y_apart, z_apart, core_apart = apart // (Z * C), apart // C % Z, apart % C
    other = (z_apart // HALF) ^ (me % C)
    chip = (z_apart % HALF) * C + (core_apart ^ other)
    level, member = found // EACH, found % EACH
    line = other * LINE + chip * EACH + member
    early = jnp.where(y_apart == 0, line, ABSENT * LINE).reshape(Y, n * NNZ)
    first = slice(EACH * NNZ, FIRST * NNZ)
    early = jnp.concatenate([early[:, first].reshape(-1), y_apart[first]])
    late = jnp.where(
        level == 0,
        y_apart * (2 * LINE) + line,
        (2 * level + other) * PLACES + (chip * Y + y_apart) * EACH + member,
    )
    return early, late.reshape(Y, n * NNZ)[:, FIRST * NNZ :].reshape(-1)


def local(right_side, lower, diag_inv, levels, columns):
    me = lax.axis_index(ROWS)
    my_x = lax.axis_index("rhs")
    rhs, inverse, own_tiles, mine = right_side[:, 0], diag_inv[:, 0], lower[:, 0, 0], columns[:, 0]
    n, width, block = rhs.shape
    part = width // Y
    kind = rhs.dtype

    def call(kernel, out, specs, operands, name, out_specs=None, **more):
        return pl.pallas_call(
            kernel,
            out_shape=out,
            in_specs=specs,
            out_specs=out_specs or ((VMEM,) * len(out) if isinstance(out, tuple) else VMEM),
            compiler_params=PARAMS,
            name=name,
            **more,
        )(*operands)

    spot = spots_of(levels)
    own = lax.dynamic_index_in_dim(spot, me, 1, keepdims=False)
    row = jnp.arange(n, dtype=jnp.int32)
    order = jnp.sum(jnp.where(own[None, :] == row[:, None], row[None, :], 0), 1)
    order = jnp.concatenate([order, jnp.stack([me // (Z * C), my_x]).astype(jnp.int32)])

    digits = jnp.concatenate([mine // BASE, mine % BASE], 1).astype(kind)
    digits = jnp.pad(digits, ((0, part - n), (0, block - 2 * NNZ)))

    payload = shape((GROUP * EACH + SHARE, block, block), kind)
    pair = shape((EACH, width, block), kind)
    square = shape((EACH, block, block), kind)
    n_copies = 2 * FIRST + LATE + EACH + GROUPS * (GROUP * EACH + SHARE)
    fresh, late_rows, rhs_early, inverse_early, early_tiles, *payloads = pl.pallas_call(
        start_kernel,
        out_shape=(pair, shape((LATE, width, block), kind), pair, square, square) + (payload,) * GROUPS,
        in_specs=[SMEM, ANY, ANY, ANY],
        out_specs=(VMEM,) * (5 + GROUPS),
        scratch_shapes=[
            pltpu.VMEM((EACH, width, block), kind),
            pltpu.VMEM((EACH, block, block), kind),
            pltpu.SemaphoreType.DMA((n_copies,)),
        ],
        name="start",
    )(order, rhs, own_tiles, inverse)
    factors = [lax.all_gather(p, ("y", "rhs"), axis=0) for p in payloads]

    def spread(held):
        tiles, rows = held
        rhs_now, inverse_now, *messages = call(
            quarter_kernel,
            (pair, square) + (shape((LATE + 1, part, block), kind),) * Y,
            [SMEM] + [VMEM] * 4,
            (order, rows, rhs_early, inverse_early, digits),
            "quarters",
        )
        over_x = [lax.ppermute(tiles, "rhs", [(i, i ^ k) for i in range(X)]) for k in range(1, X)]
        return jnp.stack([tiles] + over_x, 0), swap_y(list(messages)), rhs_now, inverse_now

    solved = [fresh]
    kept, (tiles, messages, rhs_early, inverse_early) = line_exchange(fresh, (early_tiles, late_rows), spread)
    read = jnp.stack([m[LATE, :n, : 2 * NNZ] for m in messages], 0).astype(jnp.int32)
    codes, late_codes = make_codes(spot, read[:, :, :NNZ] * BASE + read[:, :, NNZ:], me)
    chosen = call(select_kernel, (shape((SLOTS, width, block), kind),) * Y, [SMEM] + [VMEM] * 2, (codes, *kept), "select")
    chosen = swap_y(list(chosen))
    fresh, *split = call(
        early_kernel,
        (shape((EACH, width, block), kind),) + (shape((EACH, part, block), kind),) * Y,
        [SMEM, SMEM] + [VMEM] * (3 + Y),
        (codes, order, rhs_early, inverse_early, tiles, *chosen),
        "level_1",
    )
    solved.append(fresh)
    oldest = call(split_kernel, (shape((2 * LINE, part, block), kind),) * Y, [SMEM] + [VMEM] * 2, (order, *kept), "split")
    lines, (oldest, factors[0]) = line_exchange(
        jnp.concatenate(swap_y(list(split)), 0), None, (swap_y(list(oldest)), factors[0])
    )
    lines = list(lines)
    late = []
    for level in range(EARLY, LEVELS):
        last = level == LEVELS - 1
        group = (level - EARLY) // GROUP
        operands = [late_codes, order, factors[group], *messages, *oldest, *lines] + (late if last else [])
        outs = call(
            functools.partial(late_kernel, level),
            (shape((LATE, part, block), kind),) * Y if last else (shape((Y * EACH, part, block), kind),),
            [SMEM, SMEM] + [VMEM] * (len(operands) - 2),
            operands,
            f"level_{level}",
            scratch_shapes=[pltpu.VMEM((2 * level, PLACES, part, block), kind)],
        )
        if not last:
            late += outs
            ends = (level + 1 - EARLY) // GROUP != group
            new, held = line_exchange(outs[0], None, factors[group + 1] if ends else None)
            if ends:
                factors[group + 1] = held
            lines += new
    pieces = swap_y(list(outs))
    out = call(gather_kernel, shape(rhs.shape, kind), [SMEM] + [VMEM] * (EARLY + Y), (order, *solved, *pieces), "gather")
    return out[:, None]


def solution(mesh):
    parts = Mesh(mesh.devices.reshape(Y, Z, C, X), ROWS + ("rhs",))
    in_specs = (
        P(None, ROWS, "rhs", None),
        P(None, ROWS, "rhs", None, None),
        P(None, ROWS, None, None),
        P(),
        P(None, ROWS, None),
    )
    out_specs = P(None, ROWS, "rhs", None)
    return jax.shard_map(local, mesh=parts, in_specs=in_specs, out_specs=out_specs, check_vma=False)
```

profile of v0, /device:TPU:1, one launch (start us, length us, event | category | flops | bytes accessed | tf_op | source)
XLA Modules:
  0.0 218.1 jit_solution(16360212303324117658)
XLA Ops:
  9.1 3.1 %start.1 = (bf16[2,64,128]{2,1,0:T(8,128)(2,1)}, bf16[12,64,128]{2,1,0:T(8,128)(2,1)}, bf16[2,64,128]{2,1,0:T(8,128)(2,1)}, bf16[2,128,128]{2,1,0:T(8,128)(2,1)}...) custom-call(s32[18]{0:T(128)} %pad_add_fusion.order, ...), custom_call_target="tpu_custom_call" | custom-call | tf_op jit(solution)/shard_map/start/pallas_call | solution.py:249
  13.0 3.3 %collective-permute-start = (bf16[2,64,128]{2,1,0:T(8,128)(2,1)}, bf16[2,64,128]{2,1,0:T(8,128)(2,1)S(1)}, u32[]{:S(2)}, u32[]{:S(2)}) collective-permute-start(bf16[2,64,128]{2,1,0:T(8,128)(2,1)} %get-tuple-element.54.refs_0_), channel_id=1, source_target_pairs={{0,4},{4,0},{8,12},{12,8},{16,20},{20,16},{24,28},{28,24},{32,36},... | collective-permute-start | bytes 98312 | tf_op jit(solution)/shard_map/ppermute | solution.py:36
  21.5 3.9 %collective-permute-start.4 = (bf16[4,64,128]{2,1,0:T(8,128)(2,1)S(1)}, bf16[4,64,128]{2,1,0:T(8,128)(2,1)S(1)}, u32[]{:S(2)}, u32[]{:S(2)}) collective-permute-start(bf16[4,64,128]{2,1,0:T(8,128)(2,1)S(1)} %pad_maximum_fusion.4), channel_id=1, source_target_pairs={{0,24},{4,60},{8,16},{12,52},{16,8},{20,44},{24,0},{28,36},{32,56}... | collective-permute-start | bytes 196616 | tf_op jit(solution)/shard_map/ppermute | solution.py:50
  29.7 3.5 %collective-permute-start.2 = (bf16[4,64,128]{2,1,0:T(8,128)(2,1)S(1)}, bf16[4,64,128]{2,1,0:T(8,128)(2,1)S(1)}, u32[]{:S(2)}, u32[]{:S(2)}) collective-permute-start(bf16[4,64,128]{2,1,0:T(8,128)(2,1)S(1)} %pad_maximum_fusion.4), channel_id=1, source_target_pairs={{0,8},{4,44},{8,0},{12,36},{16,24},{20,60},{24,16},{28,52},{32,40}... | collective-permute-start | bytes 196616 | tf_op jit(solution)/shard_map/ppermute | solution.py:50
  33.2 3.7 %collective-permute-start.1 = (bf16[4,64,128]{2,1,0:T(8,128)(2,1)S(1)}, bf16[4,64,128]{2,1,0:T(8,128)(2,1)S(1)}, u32[]{:S(2)}, u32[]{:S(2)}) collective-permute-start(bf16[4,64,128]{2,1,0:T(8,128)(2,1)S(1)} %pad_maximum_fusion.4), channel_id=1, source_target_pairs={{0,0},{4,36},{8,8},{12,44},{16,16},{20,52},{24,24},{28,60},{32,32}... | collective-permute-start | bytes 196616 | tf_op jit(solution)/shard_map/ppermute | solution.py:50
  55.8 3.6 %collective-permute-done.13.refs_2_ = bf16[8,64,128]{2,1,0:T(8,128)(2,1)S(1)} collective-permute-done((bf16[8,64,128]{2,1,0:T(8,128)(2,1)S(1)}, bf16[8,64,128]{2,1,0:T(8,128)(2,1)S(1)}, u32[]{:S(2)}, u32[]{:S(2)}) %collective-permute-start.13) | collective-permute-done | bytes 131104 | tf_op jit(solution)/shard_map/ppermute | solution.py:36
  59.4 3.7 %collective-permute-done.14.refs_3_ = bf16[8,64,128]{2,1,0:T(8,128)(2,1)S(1)} collective-permute-done((bf16[8,64,128]{2,1,0:T(8,128)(2,1)S(1)}, bf16[8,64,128]{2,1,0:T(8,128)(2,1)S(1)}, u32[]{:S(2)}, u32[]{:S(2)}) %collective-permute-start.14) | collective-permute-done | bytes 131104 | tf_op jit(solution)/shard_map/ppermute | solution.py:36
  64.3 4.1 %collective-permute-start.16 = (bf16[2,16,128]{2,1,0:T(8,128)(2,1)S(1)}, bf16[2,16,128]{2,1,0:T(8,128)(2,1)S(1)}, u32[]{:S(2)}, u32[]{:S(2)}) collective-permute-start(bf16[2,16,128]{2,1,0:T(8,128)(2,1)S(1)} %get-tuple-element.83), channel_id=1, source_target_pairs={{0,128},{4,132},{8,136},{12,140},{16,144},{20,148},{24,152},{28,15... | collective-permute-start | bytes 24584 | tf_op jit(solution)/shard_map/ppermute | solution.py:36
  69.7 3.0 %collective-permute-done.17 = bf16[2,16,128]{2,1,0:T(8,128)(2,1)S(1)} collective-permute-done((bf16[2,16,128]{2,1,0:T(8,128)(2,1)S(1)}, bf16[2,16,128]{2,1,0:T(8,128)(2,1)S(1)}, u32[]{:S(2)}, u32[]{:S(2)}) %collective-permute-start.17) | collective-permute-done | bytes 8224 | tf_op jit(solution)/shard_map/ppermute | solution.py:36
  72.7 2.9 %collective-permute-start.18 = (bf16[8,16,128]{2,1,0:T(8,128)(2,1)S(1)}, bf16[8,16,128]{2,1,0:T(8,128)(2,1)S(1)}, u32[]{:S(2)}, u32[]{:S(2)}) collective-permute-start(bf16[8,16,128]{2,1,0:T(8,128)(2,1)S(1)} %pad_maximum_fusion.10), channel_id=1, source_target_pairs={{0,4},{4,0},{8,12},{12,8},{16,20},{20,16},{24,28},{28,24},{32,36},... | collective-permute-start | bytes 98312 | tf_op jit(solution)/shard_map/ppermute | solution.py:36
  82.0 5.3 %collective-permute-start.19 = (bf16[16,16,128]{2,1,0:T(8,128)(2,1)S(1)}, bf16[16,16,128]{2,1,0:T(8,128)(2,1)S(1)}, u32[]{:S(2)}, u32[]{:S(2)}) collective-permute-start(bf16[16,16,128]{2,1,0:T(8,128)(2,1)S(1)} %constant_dynamic-update-slice_fusion), channel_id=1, source_target_pairs={{0,0},{4,36},{8,8},{12,44},{16,16},{20,52},{24,24},{28,60},{32,32}... | collective-permute-start | bytes 196616 | tf_op jit(solution)/shard_map/ppermute | solution.py:50
  88.8 3.0 %collective-permute-start.25 = (bf16[32,16,128]{2,1,0:T(8,128)(2,1)S(1)}, bf16[32,16,128]{2,1,0:T(8,128)(2,1)S(1)}, u32[]{:S(2)}, u32[]{:S(2)}) collective-permute-start(bf16[32,16,128]{2,1,0:T(8,128)(2,1)S(1)} %get-tuple-element.88), channel_id=1, source_target_pairs={{0,192},{4,196},{8,200},{12,204},{16,208},{20,212},{24,216},{28,22... | collective-permute-start | bytes 393224 | tf_op jit(solution)/shard_map/ppermute | solution.py:36
  101.9 4.5 %collective-permute-start.28 = (bf16[16,16,128]{2,1,0:T(8,128)(2,1)S(1)}, bf16[16,16,128]{2,1,0:T(8,128)(2,1)S(1)}, u32[]{:S(2)}, u32[]{:S(2)}) collective-permute-start(bf16[16,16,128]{2,1,0:T(8,128)(2,1)S(1)} %pad_maximum_fusion.5), channel_id=1, source_target_pairs={{0,0},{4,36},{8,8},{12,44},{16,16},{20,52},{24,24},{28,60},{32,32}... | collective-permute-start | bytes 196616 | tf_op jit(solution)/shard_map/ppermute | solution.py:50
  112.0 3.2 %collective-permute-done.29 = bf16[16,16,128]{2,1,0:T(8,128)(2,1)S(1)} collective-permute-done((bf16[16,16,128]{2,1,0:T(8,128)(2,1)S(1)}, bf16[16,16,128]{2,1,0:T(8,128)(2,1)S(1)}, u32[]{:S(2)}, u32[]{:S(2)}) %collective-permute-start.29) | collective-permute-done | bytes 65568 | tf_op jit(solution)/shard_map/ppermute | solution.py:50
  121.2 4.1 %collective-permute-start.34 = (bf16[16,16,128]{2,1,0:T(8,128)(2,1)S(1)}, bf16[16,16,128]{2,1,0:T(8,128)(2,1)S(1)}, u32[]{:S(2)}, u32[]{:S(2)}) collective-permute-start(bf16[16,16,128]{2,1,0:T(8,128)(2,1)S(1)} %pad_maximum_fusion.6), channel_id=1, source_target_pairs={{0,0},{4,36},{8,8},{12,44},{16,16},{20,52},{24,24},{28,60},{32,32}... | collective-permute-start | bytes 196616 | tf_op jit(solution)/shard_map/ppermute | solution.py:50
  125.3 5.2 %collective-permute-start.35 = (bf16[16,16,128]{2,1,0:T(8,128)(2,1)S(1)}, bf16[16,16,128]{2,1,0:T(8,128)(2,1)S(1)}, u32[]{:S(2)}, u32[]{:S(2)}) collective-permute-start(bf16[16,16,128]{2,1,0:T(8,128)(2,1)S(1)} %pad_maximum_fusion.6), channel_id=1, source_target_pairs={{0,8},{4,44},{8,0},{12,36},{16,24},{20,60},{24,16},{28,52},{32,40}... | collective-permute-start | bytes 196616 | tf_op jit(solution)/shard_map/ppermute | solution.py:50
  143.0 3.3 %collective-permute-start.42 = (bf16[16,16,128]{2,1,0:T(8,128)(2,1)S(1)}, bf16[16,16,128]{2,1,0:T(8,128)(2,1)S(1)}, u32[]{:S(2)}, u32[]{:S(2)}) collective-permute-start(bf16[16,16,128]{2,1,0:T(8,128)(2,1)S(1)} %pad_maximum_fusion.7), channel_id=1, source_target_pairs={{0,16},{4,52},{8,24},{12,60},{16,0},{20,36},{24,8},{28,44},{32,48}... | collective-permute-start | bytes 196616 | tf_op jit(solution)/shard_map/ppermute | solution.py:50
  146.9 5.9 %collective-permute-start.40 = (bf16[16,16,128]{2,1,0:T(8,128)(2,1)S(1)}, bf16[16,16,128]{2,1,0:T(8,128)(2,1)S(1)}, u32[]{:S(2)}, u32[]{:S(2)}) collective-permute-start(bf16[16,16,128]{2,1,0:T(8,128)(2,1)S(1)} %pad_maximum_fusion.7), channel_id=1, source_target_pairs={{0,0},{4,36},{8,8},{12,44},{16,16},{20,52},{24,24},{28,60},{32,32}... | collective-permute-start | bytes 196616 | tf_op jit(solution)/shard_map/ppermute | solution.py:50
  152.9 2.9 %collective-permute-done.40 = bf16[16,16,128]{2,1,0:T(8,128)(2,1)S(1)} collective-permute-done((bf16[16,16,128]{2,1,0:T(8,128)(2,1)S(1)}, bf16[16,16,128]{2,1,0:T(8,128)(2,1)S(1)}, u32[]{:S(2)}, u32[]{:S(2)}) %collective-permute-start.40) | collective-permute-done | bytes 65568 | tf_op jit(solution)/shard_map/ppermute | solution.py:50
  163.2 5.9 %collective-permute-start.46 = (bf16[16,16,128]{2,1,0:T(8,128)(2,1)S(1)}, bf16[16,16,128]{2,1,0:T(8,128)(2,1)S(1)}, u32[]{:S(2)}, u32[]{:S(2)}) collective-permute-start(bf16[16,16,128]{2,1,0:T(8,128)(2,1)S(1)} %pad_maximum_fusion.8), channel_id=1, source_target_pairs={{0,0},{4,36},{8,8},{12,44},{16,16},{20,52},{24,24},{28,60},{32,32}... | collective-permute-start | bytes 196616 | tf_op jit(solution)/shard_map/ppermute | solution.py:50
  169.1 3.9 %collective-permute-start.47 = (bf16[16,16,128]{2,1,0:T(8,128)(2,1)S(1)}, bf16[16,16,128]{2,1,0:T(8,128)(2,1)S(1)}, u32[]{:S(2)}, u32[]{:S(2)}) collective-permute-start(bf16[16,16,128]{2,1,0:T(8,128)(2,1)S(1)} %pad_maximum_fusion.8), channel_id=1, source_target_pairs={{0,8},{4,44},{8,0},{12,36},{16,24},{20,60},{24,16},{28,52},{32,40}... | collective-permute-start | bytes 196616 | tf_op jit(solution)/shard_map/ppermute | solution.py:50
  183.4 5.0 %collective-permute-start.52 = (bf16[16,16,128]{2,1,0:T(8,128)(2,1)S(1)}, bf16[16,16,128]{2,1,0:T(8,128)(2,1)S(1)}, u32[]{:S(2)}, u32[]{:S(2)}) collective-permute-start(bf16[16,16,128]{2,1,0:T(8,128)(2,1)S(1)} %pad_maximum_fusion.9), channel_id=1, source_target_pairs={{0,0},{4,36},{8,8},{12,44},{16,16},{20,52},{24,24},{28,60},{32,32}... | collective-permute-start | bytes 196616 | tf_op jit(solution)/shard_map/ppermute | solution.py:50
  188.4 3.1 %collective-permute-start.53 = (bf16[16,16,128]{2,1,0:T(8,128)(2,1)S(1)}, bf16[16,16,128]{2,1,0:T(8,128)(2,1)S(1)}, u32[]{:S(2)}, u32[]{:S(2)}) collective-permute-start(bf16[16,16,128]{2,1,0:T(8,128)(2,1)S(1)} %pad_maximum_fusion.9), channel_id=1, source_target_pairs={{0,8},{4,44},{8,0},{12,36},{16,24},{20,60},{24,16},{28,52},{32,40}... | collective-permute-start | bytes 196616 | tf_op jit(solution)/shard_map/ppermute | solution.py:50
  202.4 3.4 %collective-permute-start.58 = (bf16[12,16,128]{2,1,0:T(8,128)(2,1)S(1)}, bf16[12,16,128]{2,1,0:T(8,128)(2,1)S(1)}, u32[]{:S(2)}, u32[]{:S(2)}) collective-permute-start(bf16[12,16,128]{2,1,0:T(8,128)(2,1)S(1)} %get-tuple-element.101), channel_id=1, source_target_pairs={{0,128},{4,132},{8,136},{12,140},{16,144},{20,148},{24,152},{28,15... | collective-permute-start | bytes 147464 | tf_op jit(solution)/shard_map/ppermute | solution.py:36
  (199 shorter events, 110.8 us)
Async XLA Ops:
  6.5 88.2 %all-gather.5.cloned.1.call-start = ((), (), s32[]{:S(2)}) async-start(), calls=%async_computation | async-start | bytes 4456448 | tf_op jit(solution)/shard_map/all_gather | solution.py:261
  12.2 143.6 %all-gather.7.cloned.1.call-start = ((), (), s32[]{:S(2)}) async-start(), calls=%async_computation.1 | async-start | bytes 4456448 | tf_op jit(solution)/shard_map/all_gather | solution.py:261
  18.2 11.5 %collective-permute-start.7 = (bf16[2,128,128]{2,1,0:T(8,128)(2,1)}, bf16[2,128,128]{2,1,0:T(8,128)(2,1)S(1)}, u32[]{:S(2)}, u32[]{:S(2)}) collective-permute-start(bf16[2,128,128]{2,1,0:T(8,128)(2,1)} %get-tuple-element.58), channel_id=1, source_target_pairs={{0,3},{1,2},{2,1},{3,0},{4,7},{5,6},{6,5},{7,4},{8,11},{9,10},{10,... | collective-permute-start | bytes 196616 | tf_op jit(solution)/shard_map/ppermute | solution.py:272
  18.9 14.3 %collective-permute-start.6 = (bf16[2,128,128]{2,1,0:T(8,128)(2,1)}, bf16[2,128,128]{2,1,0:T(8,128)(2,1)S(1)}, u32[]{:S(2)}, u32[]{:S(2)}) collective-permute-start(bf16[2,128,128]{2,1,0:T(8,128)(2,1)} %get-tuple-element.58), channel_id=1, source_target_pairs={{0,2},{1,3},{2,0},{3,1},{4,6},{5,7},{6,4},{7,5},{8,10},{9,11},{10,... | collective-permute-start | bytes 196616 | tf_op jit(solution)/shard_map/ppermute | solution.py:272
  19.4 17.5 %collective-permute-start.5 = (bf16[2,128,128]{2,1,0:T(8,128)(2,1)}, bf16[2,128,128]{2,1,0:T(8,128)(2,1)S(1)}, u32[]{:S(2)}, u32[]{:S(2)}) collective-permute-start(bf16[2,128,128]{2,1,0:T(8,128)(2,1)} %get-tuple-element.58), channel_id=1, source_target_pairs={{0,1},{1,0},{2,3},{3,2},{4,5},{5,4},{6,7},{7,6},{8,9},{9,8},{10,11... | collective-permute-start | bytes 196616 | tf_op jit(solution)/shard_map/ppermute | solution.py:272
  21.5 17.7 %collective-permute-start.4 = (bf16[4,64,128]{2,1,0:T(8,128)(2,1)S(1)}, bf16[4,64,128]{2,1,0:T(8,128)(2,1)S(1)}, u32[]{:S(2)}, u32[]{:S(2)}) collective-permute-start(bf16[4,64,128]{2,1,0:T(8,128)(2,1)S(1)} %pad_maximum_fusion.4), channel_id=1, source_target_pairs={{0,24},{4,60},{8,16},{12,52},{16,8},{20,44},{24,0},{28,36},{32,56}... | collective-permute-start | bytes 196616 | tf_op jit(solution)/shard_map/ppermute | solution.py:50
  25.4 16.6 %collective-permute-start.3 = (bf16[4,64,128]{2,1,0:T(8,128)(2,1)S(1)}, bf16[4,64,128]{2,1,0:T(8,128)(2,1)S(1)}, u32[]{:S(2)}, u32[]{:S(2)}) collective-permute-start(bf16[4,64,128]{2,1,0:T(8,128)(2,1)S(1)} %pad_maximum_fusion.4), channel_id=1, source_target_pairs={{0,16},{4,52},{8,24},{12,60},{16,0},{20,36},{24,8},{28,44},{32,48}... | collective-permute-start | bytes 196616 | tf_op jit(solution)/shard_map/ppermute | solution.py:50
  29.7 12.3 %collective-permute-start.2 = (bf16[4,64,128]{2,1,0:T(8,128)(2,1)S(1)}, bf16[4,64,128]{2,1,0:T(8,128)(2,1)S(1)}, u32[]{:S(2)}, u32[]{:S(2)}) collective-permute-start(bf16[4,64,128]{2,1,0:T(8,128)(2,1)S(1)} %pad_maximum_fusion.4), channel_id=1, source_target_pairs={{0,8},{4,44},{8,0},{12,36},{16,24},{20,60},{24,16},{28,52},{32,40}... | collective-permute-start | bytes 196616 | tf_op jit(solution)/shard_map/ppermute | solution.py:50
  33.2 9.6 %collective-permute-start.1 = (bf16[4,64,128]{2,1,0:T(8,128)(2,1)S(1)}, bf16[4,64,128]{2,1,0:T(8,128)(2,1)S(1)}, u32[]{:S(2)}, u32[]{:S(2)}) collective-permute-start(bf16[4,64,128]{2,1,0:T(8,128)(2,1)S(1)} %pad_maximum_fusion.4), channel_id=1, source_target_pairs={{0,0},{4,36},{8,8},{12,44},{16,16},{20,52},{24,24},{28,60},{32,32}... | collective-permute-start | bytes 196616 | tf_op jit(solution)/shard_map/ppermute | solution.py:50
  50.3 9.1 %collective-permute-start.13 = (bf16[8,64,128]{2,1,0:T(8,128)(2,1)S(1)}, bf16[8,64,128]{2,1,0:T(8,128)(2,1)S(1)}, u32[]{:S(2)}, u32[]{:S(2)}) collective-permute-start(bf16[8,64,128]{2,1,0:T(8,128)(2,1)S(1)} %get-tuple-element.78), channel_id=1, source_target_pairs={{0,128},{4,132},{8,136},{12,140},{16,144},{20,148},{24,152},{28,15... | collective-permute-start | bytes 393224 | tf_op jit(solution)/shard_map/ppermute | solution.py:36
  51.6 11.5 %collective-permute-start.14 = (bf16[8,64,128]{2,1,0:T(8,128)(2,1)S(1)}, bf16[8,64,128]{2,1,0:T(8,128)(2,1)S(1)}, u32[]{:S(2)}, u32[]{:S(2)}) collective-permute-start(bf16[8,64,128]{2,1,0:T(8,128)(2,1)S(1)} %get-tuple-element.79), channel_id=1, source_target_pairs={{0,192},{4,196},{8,200},{12,204},{16,208},{20,212},{24,216},{28,22... | collective-permute-start | bytes 393224 | tf_op jit(solution)/shard_map/ppermute | solution.py:36
  76.4 11.5 %collective-permute-start.22 = (bf16[16,16,128]{2,1,0:T(8,128)(2,1)S(1)}, bf16[16,16,128]{2,1,0:T(8,128)(2,1)S(1)}, u32[]{:S(2)}, u32[]{:S(2)}) collective-permute-start(bf16[16,16,128]{2,1,0:T(8,128)(2,1)S(1)} %constant_dynamic-update-slice_fusion), channel_id=1, source_target_pairs={{0,24},{4,60},{8,16},{12,52},{16,8},{20,44},{24,0},{28,36},{32,56}... | collective-permute-start | bytes 196616 | tf_op jit(solution)/shard_map/ppermute | solution.py:50
  78.4 10.5 %collective-permute-start.21 = (bf16[16,16,128]{2,1,0:T(8,128)(2,1)S(1)}, bf16[16,16,128]{2,1,0:T(8,128)(2,1)S(1)}, u32[]{:S(2)}, u32[]{:S(2)}) collective-permute-start(bf16[16,16,128]{2,1,0:T(8,128)(2,1)S(1)} %constant_dynamic-update-slice_fusion), channel_id=1, source_target_pairs={{0,16},{4,52},{8,24},{12,60},{16,0},{20,36},{24,8},{28,44},{32,48}... | collective-permute-start | bytes 196616 | tf_op jit(solution)/shard_map/ppermute | solution.py:50
  80.0 11.8 %collective-permute-start.20 = (bf16[16,16,128]{2,1,0:T(8,128)(2,1)S(1)}, bf16[16,16,128]{2,1,0:T(8,128)(2,1)S(1)}, u32[]{:S(2)}, u32[]{:S(2)}) collective-permute-start(bf16[16,16,128]{2,1,0:T(8,128)(2,1)S(1)} %constant_dynamic-update-slice_fusion), channel_id=1, source_target_pairs={{0,8},{4,44},{8,0},{12,36},{16,24},{20,60},{24,16},{28,52},{32,40}... | collective-permute-start | bytes 196616 | tf_op jit(solution)/shard_map/ppermute | solution.py:50
  82.0 9.8 %collective-permute-start.19 = (bf16[16,16,128]{2,1,0:T(8,128)(2,1)S(1)}, bf16[16,16,128]{2,1,0:T(8,128)(2,1)S(1)}, u32[]{:S(2)}, u32[]{:S(2)}) collective-permute-start(bf16[16,16,128]{2,1,0:T(8,128)(2,1)S(1)} %constant_dynamic-update-slice_fusion), channel_id=1, source_target_pairs={{0,0},{4,36},{8,8},{12,44},{16,16},{20,52},{24,24},{28,60},{32,32}... | collective-permute-start | bytes 196616 | tf_op jit(solution)/shard_map/ppermute | solution.py:50
  101.9 10.1 %collective-permute-start.28 = (bf16[16,16,128]{2,1,0:T(8,128)(2,1)S(1)}, bf16[16,16,128]{2,1,0:T(8,128)(2,1)S(1)}, u32[]{:S(2)}, u32[]{:S(2)}) collective-permute-start(bf16[16,16,128]{2,1,0:T(8,128)(2,1)S(1)} %pad_maximum_fusion.5), channel_id=1, source_target_pairs={{0,0},{4,36},{8,8},{12,44},{16,16},{20,52},{24,24},{28,60},{32,32}... | collective-permute-start | bytes 196616 | tf_op jit(solution)/shard_map/ppermute | solution.py:50
  106.4 8.8 %collective-permute-start.29 = (bf16[16,16,128]{2,1,0:T(8,128)(2,1)S(1)}, bf16[16,16,128]{2,1,0:T(8,128)(2,1)S(1)}, u32[]{:S(2)}, u32[]{:S(2)}) collective-permute-start(bf16[16,16,128]{2,1,0:T(8,128)(2,1)S(1)} %pad_maximum_fusion.5), channel_id=1, source_target_pairs={{0,8},{4,44},{8,0},{12,36},{16,24},{20,60},{24,16},{28,52},{32,40}... | collective-permute-start | bytes 196616 | tf_op jit(solution)/shard_map/ppermute | solution.py:50
  121.2 10.1 %collective-permute-start.34 = (bf16[16,16,128]{2,1,0:T(8,128)(2,1)S(1)}, bf16[16,16,128]{2,1,0:T(8,128)(2,1)S(1)}, u32[]{:S(2)}, u32[]{:S(2)}) collective-permute-start(bf16[16,16,128]{2,1,0:T(8,128)(2,1)S(1)} %pad_maximum_fusion.6), channel_id=1, source_target_pairs={{0,0},{4,36},{8,8},{12,44},{16,16},{20,52},{24,24},{28,60},{32,32}... | collective-permute-start | bytes 196616 | tf_op jit(solution)/shard_map/ppermute | solution.py:50
  125.3 8.0 %collective-permute-start.35 = (bf16[16,16,128]{2,1,0:T(8,128)(2,1)S(1)}, bf16[16,16,128]{2,1,0:T(8,128)(2,1)S(1)}, u32[]{:S(2)}, u32[]{:S(2)}) collective-permute-start(bf16[16,16,128]{2,1,0:T(8,128)(2,1)S(1)} %pad_maximum_fusion.6), channel_id=1, source_target_pairs={{0,8},{4,44},{8,0},{12,36},{16,24},{20,60},{24,16},{28,52},{32,40}... | collective-permute-start | bytes 196616 | tf_op jit(solution)/shard_map/ppermute | solution.py:50
  141.0 11.8 %collective-permute-start.43 = (bf16[16,16,128]{2,1,0:T(8,128)(2,1)S(1)}, bf16[16,16,128]{2,1,0:T(8,128)(2,1)S(1)}, u32[]{:S(2)}, u32[]{:S(2)}) collective-permute-start(bf16[16,16,128]{2,1,0:T(8,128)(2,1)S(1)} %pad_maximum_fusion.7), channel_id=1, source_target_pairs={{0,24},{4,60},{8,16},{12,52},{16,8},{20,44},{24,0},{28,36},{32,56}... | collective-permute-start | bytes 196616 | tf_op jit(solution)/shard_map/ppermute | solution.py:50
  143.0 9.9 %collective-permute-start.42 = (bf16[16,16,128]{2,1,0:T(8,128)(2,1)S(1)}, bf16[16,16,128]{2,1,0:T(8,128)(2,1)S(1)}, u32[]{:S(2)}, u32[]{:S(2)}) collective-permute-start(bf16[16,16,128]{2,1,0:T(8,128)(2,1)S(1)} %pad_maximum_fusion.7), channel_id=1, source_target_pairs={{0,16},{4,52},{8,24},{12,60},{16,0},{20,36},{24,8},{28,44},{32,48}... | collective-permute-start | bytes 196616 | tf_op jit(solution)/shard_map/ppermute | solution.py:50
  146.9 8.9 %collective-permute-start.40 = (bf16[16,16,128]{2,1,0:T(8,128)(2,1)S(1)}, bf16[16,16,128]{2,1,0:T(8,128)(2,1)S(1)}, u32[]{:S(2)}, u32[]{:S(2)}) collective-permute-start(bf16[16,16,128]{2,1,0:T(8,128)(2,1)S(1)} %pad_maximum_fusion.7), channel_id=1, source_target_pairs={{0,0},{4,36},{8,8},{12,44},{16,16},{20,52},{24,24},{28,60},{32,32}... | collective-permute-start | bytes 196616 | tf_op jit(solution)/shard_map/ppermute | solution.py:50
  163.2 10.2 %collective-permute-start.46 = (bf16[16,16,128]{2,1,0:T(8,128)(2,1)S(1)}, bf16[16,16,128]{2,1,0:T(8,128)(2,1)S(1)}, u32[]{:S(2)}, u32[]{:S(2)}) collective-permute-start(bf16[16,16,128]{2,1,0:T(8,128)(2,1)S(1)} %pad_maximum_fusion.8), channel_id=1, source_target_pairs={{0,0},{4,36},{8,8},{12,44},{16,16},{20,52},{24,24},{28,60},{32,32}... | collective-permute-start | bytes 196616 | tf_op jit(solution)/shard_map/ppermute | solution.py:50
  183.4 10.9 %collective-permute-start.52 = (bf16[16,16,128]{2,1,0:T(8,128)(2,1)S(1)}, bf16[16,16,128]{2,1,0:T(8,128)(2,1)S(1)}, u32[]{:S(2)}, u32[]{:S(2)}) collective-permute-start(bf16[16,16,128]{2,1,0:T(8,128)(2,1)S(1)} %pad_maximum_fusion.9), channel_id=1, source_target_pairs={{0,0},{4,36},{8,8},{12,44},{16,16},{20,52},{24,24},{28,60},{32,32}... | collective-permute-start | bytes 196616 | tf_op jit(solution)/shard_map/ppermute | solution.py:50
  (47 other events, 252.1 us)
Sparse Core Ops, SparseCore 0:
  12.4 66.1 all-gather.4
  81.0 55.5 all-gather.6
where the time goes:
time: 221 us; the launch traced here: 218 us
  starting transfers between devices  106 us (48%)
  waiting for transfers between devices  61.6 us (28%)
  Pallas kernels  21.3 us (10%)
  between operations  13.9 us (6%)
  local copies, waits for them, and re-layouts  9.67 us (4%)
  other arithmetic  5.32 us (2%)
    ppermute x28, starting transfers between devices, line_exchange(): line.append(lax.ppermute(chip, ROWS, pairs))  75.4 us
    ppermute x29, waiting for transfers between devices, swap(): return lax.ppermute(x, ROWS, [(i, i ^ mask) for i in range(Y * Z * C)])  39.5 us
    ppermute x29, starting transfers between devices, swap(): return lax.ppermute(x, ROWS, [(i, i ^ mask) for i in range(Y * Z * C)])  27.7 us
    ppermute x28, waiting for transfers between devices, line_exchange(): line.append(lax.ppermute(chip, ROWS, pairs))  21.4 us
    pallas_call x11, Pallas kernels, call(): pl.pallas_call(kernel, out_shape=out, in_specs=specs, out_specs=out_specs...  18.1 us
    unnamed x34, local copies, waits for them, and re-layouts  7.72 us
  transfers between devices with their start and end apart: 62, of which 35 were waited for; matrix products, arithmetic and copies ran while one was open for 2% of the time, Pallas kernels for 5%

commit v1 on v0

--- a/solution.py
+++ b/solution.py
@@ -46,7 +46,8 @@
         chip, after = lax.optimization_barrier((chip, after))
     line = []
     for k in range(HALF):
-        pairs = [(i, i ^ ((HALF * (i % C) + k) << 1)) for i in range(Y * Z * C)]
+        far = HALF + (HALF - k) % HALF
+        pairs = [(i, i ^ ((far if i % C else k) << 1)) for i in range(Y * Z * C)]
         line.append(lax.ppermute(chip, ROWS, pairs))
     half = jnp.concatenate(line, 0)
     if beside is not None:
@@ -200,7 +201,8 @@
     apart = (wanted % count) ^ me
     y_apart, z_apart, core_apart = apart // (Z * C), apart // C % Z, apart % C
     other = (z_apart // HALF) ^ (me % C)
-    chip = (z_apart % HALF) * C + (core_apart ^ other)
+    turn = jnp.where(z_apart < HALF, z_apart, (Z - z_apart) % HALF)
+    chip = turn * C + (core_apart ^ other)
     level, member = found // EACH, found % EACH
     line = other * LINE + chip * EACH + member
     early = jnp.where(y_apart == 0, line, ABSENT * LINE).reshape(Y, n * NNZ)

time: 221 us -> 221 us (level)
  transfers between devices with their start and end apart: 62 -> 62, of which waited for: 35 -> 36; matrix products, arithmetic and copies ran while one was open for 2% -> 2% of each run, Pallas kernels for 5% -> 5%
where the time goes in v1:
time: 221 us; the launch traced here: 219 us
  starting transfers between devices  107 us (48%)
  waiting for transfers between devices  62.2 us (28%)
  Pallas kernels  21.2 us (10%)
  between operations  13.9 us (6%)
  local copies, waits for them, and re-layouts  9.64 us (4%)
  other arithmetic  5.34 us (2%)
    ppermute x28, starting transfers between devices, line_exchange(): line.append(lax.ppermute(chip, ROWS, pairs))  75.3 us
    ppermute x29, waiting for transfers between devices, swap(): return lax.ppermute(x, ROWS, [(i, i ^ mask) for i in range(Y * Z * C)])  39 us
    ppermute x29, starting transfers between devices, swap(): return lax.ppermute(x, ROWS, [(i, i ^ mask) for i in range(Y * Z * C)])  28.1 us
    ppermute x28, waiting for transfers between devices, line_exchange(): line.append(lax.ppermute(chip, ROWS, pairs))  22.4 us
    pallas_call x11, Pallas kernels, call(): pl.pallas_call(kernel, out_shape=out, in_specs=specs, out_specs=out_specs...  18.1 us
    unnamed x34, local copies, waits for them, and re-layouts  7.69 us
  transfers between devices with their start and end apart: 62, of which 36 were waited for; matrix products, arithmetic and copies ran while one was open for 2% of the time, Pallas kernels for 5%

profile of v1, /device:TPU:1, one launch (start us, length us, event | category | flops | bytes accessed | tf_op | source)
XLA Modules:
  0.0 219.0 jit_solution(17549486011228918135)
XLA Ops:
  9.1 3.1 %start.1 = (bf16[2,64,128]{2,1,0:T(8,128)(2,1)}, bf16[12,64,128]{2,1,0:T(8,128)(2,1)}, bf16[2,64,128]{2,1,0:T(8,128)(2,1)}, bf16[2,128,128]{2,1,0:T(8,128)(2,1)}...) custom-call(s32[18]{0:T(128)} %pad_add_fusion.order, ...), custom_call_target="tpu_custom_call" | custom-call | tf_op jit(solution)/shard_map/start/pallas_call | solution.py:251
  13.0 3.3 %collective-permute-start = (bf16[2,64,128]{2,1,0:T(8,128)(2,1)}, bf16[2,64,128]{2,1,0:T(8,128)(2,1)S(1)}, u32[]{:S(2)}, u32[]{:S(2)}) collective-permute-start(bf16[2,64,128]{2,1,0:T(8,128)(2,1)} %get-tuple-element.54.refs_0_), channel_id=1, source_target_pairs={{0,4},{4,0},{8,12},{12,8},{16,20},{20,16},{24,28},{28,24},{32,36},... | collective-permute-start | bytes 98312 | tf_op jit(solution)/shard_map/ppermute | solution.py:36
  21.5 4.8 %collective-permute-start.4 = (bf16[4,64,128]{2,1,0:T(8,128)(2,1)S(1)}, bf16[4,64,128]{2,1,0:T(8,128)(2,1)S(1)}, u32[]{:S(2)}, u32[]{:S(2)}) collective-permute-start(bf16[4,64,128]{2,1,0:T(8,128)(2,1)S(1)} %pad_maximum_fusion.4), channel_id=1, source_target_pairs={{0,24},{4,44},{8,16},{12,36},{16,8},{20,60},{24,0},{28,52},{32,56}... | collective-permute-start | bytes 196616 | tf_op jit(solution)/shard_map/ppermute | solution.py:51
  30.3 2.9 %collective-permute-start.2 = (bf16[4,64,128]{2,1,0:T(8,128)(2,1)S(1)}, bf16[4,64,128]{2,1,0:T(8,128)(2,1)S(1)}, u32[]{:S(2)}, u32[]{:S(2)}) collective-permute-start(bf16[4,64,128]{2,1,0:T(8,128)(2,1)S(1)} %pad_maximum_fusion.4), channel_id=1, source_target_pairs={{0,8},{4,60},{8,0},{12,52},{16,24},{20,44},{24,16},{28,36},{32,40}... | collective-permute-start | bytes 196616 | tf_op jit(solution)/shard_map/ppermute | solution.py:51
  33.2 3.3 %collective-permute-start.1 = (bf16[4,64,128]{2,1,0:T(8,128)(2,1)S(1)}, bf16[4,64,128]{2,1,0:T(8,128)(2,1)S(1)}, u32[]{:S(2)}, u32[]{:S(2)}) collective-permute-start(bf16[4,64,128]{2,1,0:T(8,128)(2,1)S(1)} %pad_maximum_fusion.4), channel_id=1, source_target_pairs={{0,0},{4,36},{8,8},{12,44},{16,16},{20,52},{24,24},{28,60},{32,32}... | collective-permute-start | bytes 196616 | tf_op jit(solution)/shard_map/ppermute | solution.py:51
  54.8 3.8 %collective-permute-done.13.refs_2_ = bf16[8,64,128]{2,1,0:T(8,128)(2,1)S(1)} collective-permute-done((bf16[8,64,128]{2,1,0:T(8,128)(2,1)S(1)}, bf16[8,64,128]{2,1,0:T(8,128)(2,1)S(1)}, u32[]{:S(2)}, u32[]{:S(2)}) %collective-permute-start.13) | collective-permute-done | bytes 131104 | tf_op jit(solution)/shard_map/ppermute | solution.py:36
  58.6 3.6 %collective-permute-done.14.refs_3_ = bf16[8,64,128]{2,1,0:T(8,128)(2,1)S(1)} collective-permute-done((bf16[8,64,128]{2,1,0:T(8,128)(2,1)S(1)}, bf16[8,64,128]{2,1,0:T(8,128)(2,1)S(1)}, u32[]{:S(2)}, u32[]{:S(2)}) %collective-permute-start.14) | collective-permute-done | bytes 131104 | tf_op jit(solution)/shard_map/ppermute | solution.py:36
  63.3 4.4 %collective-permute-start.16 = (bf16[2,16,128]{2,1,0:T(8,128)(2,1)S(1)}, bf16[2,16,128]{2,1,0:T(8,128)(2,1)S(1)}, u32[]{:S(2)}, u32[]{:S(2)}) collective-permute-start(bf16[2,16,128]{2,1,0:T(8,128)(2,1)S(1)} %get-tuple-element.83), channel_id=1, source_target_pairs={{0,128},{4,132},{8,136},{12,140},{16,144},{20,148},{24,152},{28,15... | collective-permute-start | bytes 24584 | tf_op jit(solution)/shard_map/ppermute | solution.py:36
  69.1 2.9 %collective-permute-done.17 = bf16[2,16,128]{2,1,0:T(8,128)(2,1)S(1)} collective-permute-done((bf16[2,16,128]{2,1,0:T(8,128)(2,1)S(1)}, bf16[2,16,128]{2,1,0:T(8,128)(2,1)S(1)}, u32[]{:S(2)}, u32[]{:S(2)}) %collective-permute-start.17) | collective-permute-done | bytes 8224 | tf_op jit(solution)/shard_map/ppermute | solution.py:36
  72.0 3.0 %collective-permute-start.18 = (bf16[8,16,128]{2,1,0:T(8,128)(2,1)S(1)}, bf16[8,16,128]{2,1,0:T(8,128)(2,1)S(1)}, u32[]{:S(2)}, u32[]{:S(2)}) collective-permute-start(bf16[8,16,128]{2,1,0:T(8,128)(2,1)S(1)} %pad_maximum_fusion.10), channel_id=1, source_target_pairs={{0,4},{4,0},{8,12},{12,8},{16,20},{20,16},{24,28},{28,24},{32,36},... | collective-permute-start | bytes 98312 | tf_op jit(solution)/shard_map/ppermute | solution.py:36
  75.9 4.4 %collective-permute-start.22 = (bf16[16,16,128]{2,1,0:T(8,128)(2,1)S(1)}, bf16[16,16,128]{2,1,0:T(8,128)(2,1)S(1)}, u32[]{:S(2)}, u32[]{:S(2)}) collective-permute-start(bf16[16,16,128]{2,1,0:T(8,128)(2,1)S(1)} %constant_dynamic-update-slice_fusion), channel_id=1, source_target_pairs={{0,24},{4,44},{8,16},{12,36},{16,8},{20,60},{24,0},{28,52},{32,56}... | collective-permute-start | bytes 196616 | tf_op jit(solution)/shard_map/ppermute | solution.py:51
  82.0 4.3 %collective-permute-start.19 = (bf16[16,16,128]{2,1,0:T(8,128)(2,1)S(1)}, bf16[16,16,128]{2,1,0:T(8,128)(2,1)S(1)}, u32[]{:S(2)}, u32[]{:S(2)}) collective-permute-start(bf16[16,16,128]{2,1,0:T(8,128)(2,1)S(1)} %constant_dynamic-update-slice_fusion), channel_id=1, source_target_pairs={{0,0},{4,36},{8,8},{12,44},{16,16},{20,52},{24,24},{28,60},{32,32}... | collective-permute-start | bytes 196616 | tf_op jit(solution)/shard_map/ppermute | solution.py:51
  87.9 2.9 %collective-permute-start.25 = (bf16[32,16,128]{2,1,0:T(8,128)(2,1)S(1)}, bf16[32,16,128]{2,1,0:T(8,128)(2,1)S(1)}, u32[]{:S(2)}, u32[]{:S(2)}) collective-permute-start(bf16[32,16,128]{2,1,0:T(8,128)(2,1)S(1)} %get-tuple-element.88), channel_id=1, source_target_pairs={{0,192},{4,196},{8,200},{12,204},{16,208},{20,212},{24,216},{28,22... | collective-permute-start | bytes 393224 | tf_op jit(solution)/shard_map/ppermute | solution.py:36
  100.9 5.4 %collective-permute-start.28 = (bf16[16,16,128]{2,1,0:T(8,128)(2,1)S(1)}, bf16[16,16,128]{2,1,0:T(8,128)(2,1)S(1)}, u32[]{:S(2)}, u32[]{:S(2)}) collective-permute-start(bf16[16,16,128]{2,1,0:T(8,128)(2,1)S(1)} %pad_maximum_fusion.5), channel_id=1, source_target_pairs={{0,0},{4,36},{8,8},{12,44},{16,16},{20,52},{24,24},{28,60},{32,32}... | collective-permute-start | bytes 196616 | tf_op jit(solution)/shard_map/ppermute | solution.py:51
  106.8 5.4 %collective-permute-start.30 = (bf16[16,16,128]{2,1,0:T(8,128)(2,1)S(1)}, bf16[16,16,128]{2,1,0:T(8,128)(2,1)S(1)}, u32[]{:S(2)}, u32[]{:S(2)}) collective-permute-start(bf16[16,16,128]{2,1,0:T(8,128)(2,1)S(1)} %pad_maximum_fusion.5), channel_id=1, source_target_pairs={{0,16},{4,52},{8,24},{12,60},{16,0},{20,36},{24,8},{28,44},{32,48}... | collective-permute-start | bytes 196616 | tf_op jit(solution)/shard_map/ppermute | solution.py:51
  114.7 4.2 %collective-permute-done.31 = bf16[16,16,128]{2,1,0:T(8,128)(2,1)S(1)} collective-permute-done((bf16[16,16,128]{2,1,0:T(8,128)(2,1)S(1)}, bf16[16,16,128]{2,1,0:T(8,128)(2,1)S(1)}, u32[]{:S(2)}, u32[]{:S(2)}) %collective-permute-start.31) | collective-permute-done | bytes 65568 | tf_op jit(solution)/shard_map/ppermute | solution.py:51
  126.3 3.6 %collective-permute-start.35 = (bf16[16,16,128]{2,1,0:T(8,128)(2,1)S(1)}, bf16[16,16,128]{2,1,0:T(8,128)(2,1)S(1)}, u32[]{:S(2)}, u32[]{:S(2)}) collective-permute-start(bf16[16,16,128]{2,1,0:T(8,128)(2,1)S(1)} %pad_maximum_fusion.6), channel_id=1, source_target_pairs={{0,8},{4,60},{8,0},{12,52},{16,24},{20,44},{24,16},{28,36},{32,40}... | collective-permute-start | bytes 196616 | tf_op jit(solution)/shard_map/ppermute | solution.py:51
  147.0 5.6 %collective-permute-start.40 = (bf16[16,16,128]{2,1,0:T(8,128)(2,1)S(1)}, bf16[16,16,128]{2,1,0:T(8,128)(2,1)S(1)}, u32[]{:S(2)}, u32[]{:S(2)}) collective-permute-start(bf16[16,16,128]{2,1,0:T(8,128)(2,1)S(1)} %pad_maximum_fusion.7), channel_id=1, source_target_pairs={{0,0},{4,36},{8,8},{12,44},{16,16},{20,52},{24,24},{28,60},{32,32}... | collective-permute-start | bytes 196616 | tf_op jit(solution)/shard_map/ppermute | solution.py:51
  152.7 3.4 %collective-permute-done.40 = bf16[16,16,128]{2,1,0:T(8,128)(2,1)S(1)} collective-permute-done((bf16[16,16,128]{2,1,0:T(8,128)(2,1)S(1)}, bf16[16,16,128]{2,1,0:T(8,128)(2,1)S(1)}, u32[]{:S(2)}, u32[]{:S(2)}) %collective-permute-start.40) | collective-permute-done | bytes 65568 | tf_op jit(solution)/shard_map/ppermute | solution.py:51
  163.4 5.6 %collective-permute-start.46 = (bf16[16,16,128]{2,1,0:T(8,128)(2,1)S(1)}, bf16[16,16,128]{2,1,0:T(8,128)(2,1)S(1)}, u32[]{:S(2)}, u32[]{:S(2)}) collective-permute-start(bf16[16,16,128]{2,1,0:T(8,128)(2,1)S(1)} %pad_maximum_fusion.8), channel_id=1, source_target_pairs={{0,0},{4,36},{8,8},{12,44},{16,16},{20,52},{24,24},{28,60},{32,32}... | collective-permute-start | bytes 196616 | tf_op jit(solution)/shard_map/ppermute | solution.py:51
  169.4 4.0 %collective-permute-start.48 = (bf16[16,16,128]{2,1,0:T(8,128)(2,1)S(1)}, bf16[16,16,128]{2,1,0:T(8,128)(2,1)S(1)}, u32[]{:S(2)}, u32[]{:S(2)}) collective-permute-start(bf16[16,16,128]{2,1,0:T(8,128)(2,1)S(1)} %pad_maximum_fusion.8), channel_id=1, source_target_pairs={{0,16},{4,52},{8,24},{12,60},{16,0},{20,36},{24,8},{28,44},{32,48}... | collective-permute-start | bytes 196616 | tf_op jit(solution)/shard_map/ppermute | solution.py:51
  176.5 3.0 %collective-permute-done.49 = bf16[16,16,128]{2,1,0:T(8,128)(2,1)S(1)} collective-permute-done((bf16[16,16,128]{2,1,0:T(8,128)(2,1)S(1)}, bf16[16,16,128]{2,1,0:T(8,128)(2,1)S(1)}, u32[]{:S(2)}, u32[]{:S(2)}) %collective-permute-start.49) | collective-permute-done | bytes 65568 | tf_op jit(solution)/shard_map/ppermute | solution.py:51
  184.7 6.4 %collective-permute-start.52 = (bf16[16,16,128]{2,1,0:T(8,128)(2,1)S(1)}, bf16[16,16,128]{2,1,0:T(8,128)(2,1)S(1)}, u32[]{:S(2)}, u32[]{:S(2)}) collective-permute-start(bf16[16,16,128]{2,1,0:T(8,128)(2,1)S(1)} %pad_maximum_fusion.9), channel_id=1, source_target_pairs={{0,0},{4,36},{8,8},{12,44},{16,16},{20,52},{24,24},{28,60},{32,32}... | collective-permute-start | bytes 196616 | tf_op jit(solution)/shard_map/ppermute | solution.py:51
  203.3 3.4 %collective-permute-start.58 = (bf16[12,16,128]{2,1,0:T(8,128)(2,1)S(1)}, bf16[12,16,128]{2,1,0:T(8,128)(2,1)S(1)}, u32[]{:S(2)}, u32[]{:S(2)}) collective-permute-start(bf16[12,16,128]{2,1,0:T(8,128)(2,1)S(1)} %get-tuple-element.101), channel_id=1, source_target_pairs={{0,128},{4,132},{8,136},{12,140},{16,144},{20,148},{24,152},{28,15... | collective-permute-start | bytes 147464 | tf_op jit(solution)/shard_map/ppermute | solution.py:36
  (200 shorter events, 108.4 us)
Async XLA Ops:
  6.5 87.3 %all-gather.5.cloned.1.call-start = ((), (), s32[]{:S(2)}) async-start(), calls=%async_computation | async-start | bytes 4456448 | tf_op jit(solution)/shard_map/all_gather | solution.py:263
  12.2 143.9 %all-gather.7.cloned.1.call-start = ((), (), s32[]{:S(2)}) async-start(), calls=%async_computation.1 | async-start | bytes 4456448 | tf_op jit(solution)/shard_map/all_gather | solution.py:263
  18.2 12.1 %collective-permute-start.7 = (bf16[2,128,128]{2,1,0:T(8,128)(2,1)}, bf16[2,128,128]{2,1,0:T(8,128)(2,1)S(1)}, u32[]{:S(2)}, u32[]{:S(2)}) collective-permute-start(bf16[2,128,128]{2,1,0:T(8,128)(2,1)} %get-tuple-element.58), channel_id=1, source_target_pairs={{0,3},{1,2},{2,1},{3,0},{4,7},{5,6},{6,5},{7,4},{8,11},{9,10},{10,... | collective-permute-start | bytes 196616 | tf_op jit(solution)/shard_map/ppermute | solution.py:274
  18.9 14.3 %collective-permute-start.6 = (bf16[2,128,128]{2,1,0:T(8,128)(2,1)}, bf16[2,128,128]{2,1,0:T(8,128)(2,1)S(1)}, u32[]{:S(2)}, u32[]{:S(2)}) collective-permute-start(bf16[2,128,128]{2,1,0:T(8,128)(2,1)} %get-tuple-element.58), channel_id=1, source_target_pairs={{0,2},{1,3},{2,0},{3,1},{4,6},{5,7},{6,4},{7,5},{8,10},{9,11},{10,... | collective-permute-start | bytes 196616 | tf_op jit(solution)/shard_map/ppermute | solution.py:274
  19.4 17.1 %collective-permute-start.5 = (bf16[2,128,128]{2,1,0:T(8,128)(2,1)}, bf16[2,128,128]{2,1,0:T(8,128)(2,1)S(1)}, u32[]{:S(2)}, u32[]{:S(2)}) collective-permute-start(bf16[2,128,128]{2,1,0:T(8,128)(2,1)} %get-tuple-element.58), channel_id=1, source_target_pairs={{0,1},{1,0},{2,3},{3,2},{4,5},{5,4},{6,7},{7,6},{8,9},{9,8},{10,11... | collective-permute-start | bytes 196616 | tf_op jit(solution)/shard_map/ppermute | solution.py:274
  21.5 17.3 %collective-permute-start.4 = (bf16[4,64,128]{2,1,0:T(8,128)(2,1)S(1)}, bf16[4,64,128]{2,1,0:T(8,128)(2,1)S(1)}, u32[]{:S(2)}, u32[]{:S(2)}) collective-permute-start(bf16[4,64,128]{2,1,0:T(8,128)(2,1)S(1)} %pad_maximum_fusion.4), channel_id=1, source_target_pairs={{0,24},{4,44},{8,16},{12,36},{16,8},{20,60},{24,0},{28,52},{32,56}... | collective-permute-start | bytes 196616 | tf_op jit(solution)/shard_map/ppermute | solution.py:51
  26.3 15.2 %collective-permute-start.3 = (bf16[4,64,128]{2,1,0:T(8,128)(2,1)S(1)}, bf16[4,64,128]{2,1,0:T(8,128)(2,1)S(1)}, u32[]{:S(2)}, u32[]{:S(2)}) collective-permute-start(bf16[4,64,128]{2,1,0:T(8,128)(2,1)S(1)} %pad_maximum_fusion.4), channel_id=1, source_target_pairs={{0,16},{4,52},{8,24},{12,60},{16,0},{20,36},{24,8},{28,44},{32,48}... | collective-permute-start | bytes 196616 | tf_op jit(solution)/shard_map/ppermute | solution.py:51
  30.3 11.2 %collective-permute-start.2 = (bf16[4,64,128]{2,1,0:T(8,128)(2,1)S(1)}, bf16[4,64,128]{2,1,0:T(8,128)(2,1)S(1)}, u32[]{:S(2)}, u32[]{:S(2)}) collective-permute-start(bf16[4,64,128]{2,1,0:T(8,128)(2,1)S(1)} %pad_maximum_fusion.4), channel_id=1, source_target_pairs={{0,8},{4,60},{8,0},{12,52},{16,24},{20,44},{24,16},{28,36},{32,40}... | collective-permute-start | bytes 196616 | tf_op jit(solution)/shard_map/ppermute | solution.py:51
  33.2 9.0 %collective-permute-start.1 = (bf16[4,64,128]{2,1,0:T(8,128)(2,1)S(1)}, bf16[4,64,128]{2,1,0:T(8,128)(2,1)S(1)}, u32[]{:S(2)}, u32[]{:S(2)}) collective-permute-start(bf16[4,64,128]{2,1,0:T(8,128)(2,1)S(1)} %pad_maximum_fusion.4), channel_id=1, source_target_pairs={{0,0},{4,36},{8,8},{12,44},{16,16},{20,52},{24,24},{28,60},{32,32}... | collective-permute-start | bytes 196616 | tf_op jit(solution)/shard_map/ppermute | solution.py:51
  49.9 8.7 %collective-permute-start.13 = (bf16[8,64,128]{2,1,0:T(8,128)(2,1)S(1)}, bf16[8,64,128]{2,1,0:T(8,128)(2,1)S(1)}, u32[]{:S(2)}, u32[]{:S(2)}) collective-permute-start(bf16[8,64,128]{2,1,0:T(8,128)(2,1)S(1)} %get-tuple-element.78), channel_id=1, source_target_pairs={{0,128},{4,132},{8,136},{12,140},{16,144},{20,148},{24,152},{28,15... | collective-permute-start | bytes 393224 | tf_op jit(solution)/shard_map/ppermute | solution.py:36
  51.2 11.0 %collective-permute-start.14 = (bf16[8,64,128]{2,1,0:T(8,128)(2,1)S(1)}, bf16[8,64,128]{2,1,0:T(8,128)(2,1)S(1)}, u32[]{:S(2)}, u32[]{:S(2)}) collective-permute-start(bf16[8,64,128]{2,1,0:T(8,128)(2,1)S(1)} %get-tuple-element.79), channel_id=1, source_target_pairs={{0,192},{4,196},{8,200},{12,204},{16,208},{20,212},{24,216},{28,22... | collective-permute-start | bytes 393224 | tf_op jit(solution)/shard_map/ppermute | solution.py:36
  75.9 11.2 %collective-permute-start.22 = (bf16[16,16,128]{2,1,0:T(8,128)(2,1)S(1)}, bf16[16,16,128]{2,1,0:T(8,128)(2,1)S(1)}, u32[]{:S(2)}, u32[]{:S(2)}) collective-permute-start(bf16[16,16,128]{2,1,0:T(8,128)(2,1)S(1)} %constant_dynamic-update-slice_fusion), channel_id=1, source_target_pairs={{0,24},{4,44},{8,16},{12,36},{16,8},{20,60},{24,0},{28,52},{32,56}... | collective-permute-start | bytes 196616 | tf_op jit(solution)/shard_map/ppermute | solution.py:51
  80.2 7.7 %collective-permute-start.21 = (bf16[16,16,128]{2,1,0:T(8,128)(2,1)S(1)}, bf16[16,16,128]{2,1,0:T(8,128)(2,1)S(1)}, u32[]{:S(2)}, u32[]{:S(2)}) collective-permute-start(bf16[16,16,128]{2,1,0:T(8,128)(2,1)S(1)} %constant_dynamic-update-slice_fusion), channel_id=1, source_target_pairs={{0,16},{4,52},{8,24},{12,60},{16,0},{20,36},{24,8},{28,44},{32,48}... | collective-permute-start | bytes 196616 | tf_op jit(solution)/shard_map/ppermute | solution.py:51
  80.2 10.6 %collective-permute-start.20 = (bf16[16,16,128]{2,1,0:T(8,128)(2,1)S(1)}, bf16[16,16,128]{2,1,0:T(8,128)(2,1)S(1)}, u32[]{:S(2)}, u32[]{:S(2)}) collective-permute-start(bf16[16,16,128]{2,1,0:T(8,128)(2,1)S(1)} %constant_dynamic-update-slice_fusion), channel_id=1, source_target_pairs={{0,8},{4,60},{8,0},{12,52},{16,24},{20,44},{24,16},{28,36},{32,40}... | collective-permute-start | bytes 196616 | tf_op jit(solution)/shard_map/ppermute | solution.py:51
  82.0 9.0 %collective-permute-start.19 = (bf16[16,16,128]{2,1,0:T(8,128)(2,1)S(1)}, bf16[16,16,128]{2,1,0:T(8,128)(2,1)S(1)}, u32[]{:S(2)}, u32[]{:S(2)}) collective-permute-start(bf16[16,16,128]{2,1,0:T(8,128)(2,1)S(1)} %constant_dynamic-update-slice_fusion), channel_id=1, source_target_pairs={{0,0},{4,36},{8,8},{12,44},{16,16},{20,52},{24,24},{28,60},{32,32}... | collective-permute-start | bytes 196616 | tf_op jit(solution)/shard_map/ppermute | solution.py:51
  100.9 11.9 %collective-permute-start.28 = (bf16[16,16,128]{2,1,0:T(8,128)(2,1)S(1)}, bf16[16,16,128]{2,1,0:T(8,128)(2,1)S(1)}, u32[]{:S(2)}, u32[]{:S(2)}) collective-permute-start(bf16[16,16,128]{2,1,0:T(8,128)(2,1)S(1)} %pad_maximum_fusion.5), channel_id=1, source_target_pairs={{0,0},{4,36},{8,8},{12,44},{16,16},{20,52},{24,24},{28,60},{32,32}... | collective-permute-start | bytes 196616 | tf_op jit(solution)/shard_map/ppermute | solution.py:51
  106.8 7.8 %collective-permute-start.30 = (bf16[16,16,128]{2,1,0:T(8,128)(2,1)S(1)}, bf16[16,16,128]{2,1,0:T(8,128)(2,1)S(1)}, u32[]{:S(2)}, u32[]{:S(2)}) collective-permute-start(bf16[16,16,128]{2,1,0:T(8,128)(2,1)S(1)} %pad_maximum_fusion.5), channel_id=1, source_target_pairs={{0,16},{4,52},{8,24},{12,60},{16,0},{20,36},{24,8},{28,44},{32,48}... | collective-permute-start | bytes 196616 | tf_op jit(solution)/shard_map/ppermute | solution.py:51
  123.9 10.1 %collective-permute-start.34 = (bf16[16,16,128]{2,1,0:T(8,128)(2,1)S(1)}, bf16[16,16,128]{2,1,0:T(8,128)(2,1)S(1)}, u32[]{:S(2)}, u32[]{:S(2)}) collective-permute-start(bf16[16,16,128]{2,1,0:T(8,128)(2,1)S(1)} %pad_maximum_fusion.6), channel_id=1, source_target_pairs={{0,0},{4,36},{8,8},{12,44},{16,16},{20,52},{24,24},{28,60},{32,32}... | collective-permute-start | bytes 196616 | tf_op jit(solution)/shard_map/ppermute | solution.py:51
  126.3 7.7 %collective-permute-start.35 = (bf16[16,16,128]{2,1,0:T(8,128)(2,1)S(1)}, bf16[16,16,128]{2,1,0:T(8,128)(2,1)S(1)}, u32[]{:S(2)}, u32[]{:S(2)}) collective-permute-start(bf16[16,16,128]{2,1,0:T(8,128)(2,1)S(1)} %pad_maximum_fusion.6), channel_id=1, source_target_pairs={{0,8},{4,60},{8,0},{12,52},{16,24},{20,44},{24,16},{28,36},{32,40}... | collective-permute-start | bytes 196616 | tf_op jit(solution)/shard_map/ppermute | solution.py:51
  142.6 10.0 %collective-permute-start.43 = (bf16[16,16,128]{2,1,0:T(8,128)(2,1)S(1)}, bf16[16,16,128]{2,1,0:T(8,128)(2,1)S(1)}, u32[]{:S(2)}, u32[]{:S(2)}) collective-permute-start(bf16[16,16,128]{2,1,0:T(8,128)(2,1)S(1)} %pad_maximum_fusion.7), channel_id=1, source_target_pairs={{0,24},{4,44},{8,16},{12,36},{16,8},{20,60},{24,0},{28,52},{32,56}... | collective-permute-start | bytes 196616 | tf_op jit(solution)/shard_map/ppermute | solution.py:51
  145.4 7.2 %collective-permute-start.42 = (bf16[16,16,128]{2,1,0:T(8,128)(2,1)S(1)}, bf16[16,16,128]{2,1,0:T(8,128)(2,1)S(1)}, u32[]{:S(2)}, u32[]{:S(2)}) collective-permute-start(bf16[16,16,128]{2,1,0:T(8,128)(2,1)S(1)} %pad_maximum_fusion.7), channel_id=1, source_target_pairs={{0,16},{4,52},{8,24},{12,60},{16,0},{20,36},{24,8},{28,44},{32,48}... | collective-permute-start | bytes 196616 | tf_op jit(solution)/shard_map/ppermute | solution.py:51
  147.0 9.0 %collective-permute-start.40 = (bf16[16,16,128]{2,1,0:T(8,128)(2,1)S(1)}, bf16[16,16,128]{2,1,0:T(8,128)(2,1)S(1)}, u32[]{:S(2)}, u32[]{:S(2)}) collective-permute-start(bf16[16,16,128]{2,1,0:T(8,128)(2,1)S(1)} %pad_maximum_fusion.7), channel_id=1, source_target_pairs={{0,0},{4,36},{8,8},{12,44},{16,16},{20,52},{24,24},{28,60},{32,32}... | collective-permute-start | bytes 196616 | tf_op jit(solution)/shard_map/ppermute | solution.py:51
  163.4 11.1 %collective-permute-start.46 = (bf16[16,16,128]{2,1,0:T(8,128)(2,1)S(1)}, bf16[16,16,128]{2,1,0:T(8,128)(2,1)S(1)}, u32[]{:S(2)}, u32[]{:S(2)}) collective-permute-start(bf16[16,16,128]{2,1,0:T(8,128)(2,1)S(1)} %pad_maximum_fusion.8), channel_id=1, source_target_pairs={{0,0},{4,36},{8,8},{12,44},{16,16},{20,52},{24,24},{28,60},{32,32}... | collective-permute-start | bytes 196616 | tf_op jit(solution)/shard_map/ppermute | solution.py:51
  184.7 10.6 %collective-permute-start.52 = (bf16[16,16,128]{2,1,0:T(8,128)(2,1)S(1)}, bf16[16,16,128]{2,1,0:T(8,128)(2,1)S(1)}, u32[]{:S(2)}, u32[]{:S(2)}) collective-permute-start(bf16[16,16,128]{2,1,0:T(8,128)(2,1)S(1)} %pad_maximum_fusion.9), channel_id=1, source_target_pairs={{0,0},{4,36},{8,8},{12,44},{16,16},{20,52},{24,24},{28,60},{32,32}... | collective-permute-start | bytes 196616 | tf_op jit(solution)/shard_map/ppermute | solution.py:51
  (47 other events, 252.9 us)
Sparse Core Ops, SparseCore 0:
  12.3 65.7 all-gather.4
  80.6 55.9 all-gather.6

commit v2 on v0

--- a/solution.py
+++ b/solution.py
@@ -234,7 +234,7 @@
         )(*operands)
 
     spot = spots_of(levels)
-    own = lax.dynamic_index_in_dim(spot, me, 1, keepdims=False)
+    own = spots_of(lax.dynamic_slice_in_dim(levels, me, 1, 1))[:, 0]
     row = jnp.arange(n, dtype=jnp.int32)
     order = jnp.sum(jnp.where(own[None, :] == row[:, None], row[None, :], 0), 1)
     order = jnp.concatenate([order, jnp.stack([me // (Z * C), my_x]).astype(jnp.int32)])

time: 221 us -> 224 us (1.014)
    unnamed x34 -> x35, local copies, waits for them, and re-layouts: 7.72 us -> 7.81 us
  transfers between devices with their start and end apart: 62 -> 62, of which waited for: 35 -> 35; matrix products, arithmetic and copies ran while one was open for 2% -> 3% of each run, Pallas kernels for 5% -> 4%
where the time goes in v2:
time: 224 us; the launch traced here: 221 us
  starting transfers between devices  107 us (48%)
  waiting for transfers between devices  63 us (28%)
  Pallas kernels  21.2 us (9%)
  between operations  13.9 us (6%)
  local copies, waits for them, and re-layouts  10.3 us (5%)
  other arithmetic  5.5 us (2%)
    ppermute x28, starting transfers between devices, line_exchange(): line.append(lax.ppermute(chip, ROWS, pairs))  75.4 us
    ppermute x29, waiting for transfers between devices, swap(): return lax.ppermute(x, ROWS, [(i, i ^ mask) for i in range(Y * Z * C)])  40.6 us
    ppermute x29, starting transfers between devices, swap(): return lax.ppermute(x, ROWS, [(i, i ^ mask) for i in range(Y * Z * C)])  28.7 us
    ppermute x28, waiting for transfers between devices, line_exchange(): line.append(lax.ppermute(chip, ROWS, pairs))  21.7 us
    pallas_call x11, Pallas kernels, call(): pl.pallas_call(kernel, out_shape=out, in_specs=specs, out_specs=out_specs...  18.1 us
    unnamed x35, local copies, waits for them, and re-layouts  7.81 us
  transfers between devices with their start and end apart: 62, of which 35 were waited for; matrix products, arithmetic and copies ran while one was open for 3% of the time, Pallas kernels for 4%

profile of v2, /device:TPU:1, one launch (start us, length us, event | category | flops | bytes accessed | tf_op | source)
XLA Modules:
  0.0 221.3 jit_solution(12086090891044723966)
XLA Ops:
  8.3 3.1 %start.1 = (bf16[2,64,128]{2,1,0:T(8,128)(2,1)}, bf16[12,64,128]{2,1,0:T(8,128)(2,1)}, bf16[2,64,128]{2,1,0:T(8,128)(2,1)}, bf16[2,128,128]{2,1,0:T(8,128)(2,1)}...) custom-call(s32[18]{0:T(128)} %pad_add_fusion.order, ...), custom_call_target="tpu_custom_call" | custom-call | tf_op jit(solution)/shard_map/start/pallas_call | solution.py:249
  12.2 3.3 %collective-permute-start = (bf16[2,64,128]{2,1,0:T(8,128)(2,1)}, bf16[2,64,128]{2,1,0:T(8,128)(2,1)S(1)}, u32[]{:S(2)}, u32[]{:S(2)}) collective-permute-start(bf16[2,64,128]{2,1,0:T(8,128)(2,1)} %get-tuple-element.54.refs_0_), channel_id=1, source_target_pairs={{0,4},{4,0},{8,12},{12,8},{16,20},{20,16},{24,28},{28,24},{32,36},... | collective-permute-start | bytes 98312 | tf_op jit(solution)/shard_map/ppermute | solution.py:36
  22.4 3.9 %collective-permute-start.4 = (bf16[4,64,128]{2,1,0:T(8,128)(2,1)S(1)}, bf16[4,64,128]{2,1,0:T(8,128)(2,1)S(1)}, u32[]{:S(2)}, u32[]{:S(2)}) collective-permute-start(bf16[4,64,128]{2,1,0:T(8,128)(2,1)S(1)} %pad_maximum_fusion.4), channel_id=1, source_target_pairs={{0,24},{4,60},{8,16},{12,52},{16,8},{20,44},{24,0},{28,36},{32,56}... | collective-permute-start | bytes 196616 | tf_op jit(solution)/shard_map/ppermute | solution.py:50
  30.5 3.5 %collective-permute-start.2 = (bf16[4,64,128]{2,1,0:T(8,128)(2,1)S(1)}, bf16[4,64,128]{2,1,0:T(8,128)(2,1)S(1)}, u32[]{:S(2)}, u32[]{:S(2)}) collective-permute-start(bf16[4,64,128]{2,1,0:T(8,128)(2,1)S(1)} %pad_maximum_fusion.4), channel_id=1, source_target_pairs={{0,8},{4,44},{8,0},{12,36},{16,24},{20,60},{24,16},{28,52},{32,40}... | collective-permute-start | bytes 196616 | tf_op jit(solution)/shard_map/ppermute | solution.py:50
  34.1 3.7 %collective-permute-start.1 = (bf16[4,64,128]{2,1,0:T(8,128)(2,1)S(1)}, bf16[4,64,128]{2,1,0:T(8,128)(2,1)S(1)}, u32[]{:S(2)}, u32[]{:S(2)}) collective-permute-start(bf16[4,64,128]{2,1,0:T(8,128)(2,1)S(1)} %pad_maximum_fusion.4), channel_id=1, source_target_pairs={{0,0},{4,36},{8,8},{12,44},{16,16},{20,52},{24,24},{28,60},{32,32}... | collective-permute-start | bytes 196616 | tf_op jit(solution)/shard_map/ppermute | solution.py:50
  55.0 3.9 %collective-permute-done.12.refs_1_ = bf16[8,64,128]{2,1,0:T(8,128)(2,1)S(1)} collective-permute-done((bf16[8,64,128]{2,1,0:T(8,128)(2,1)S(1)}, bf16[8,64,128]{2,1,0:T(8,128)(2,1)S(1)}, u32[]{:S(2)}, u32[]{:S(2)}) %collective-permute-start.12) | collective-permute-done | bytes 131104 | tf_op jit(solution)/shard_map/ppermute | solution.py:36
  58.9 3.0 %collective-permute-done.13.refs_2_ = bf16[8,64,128]{2,1,0:T(8,128)(2,1)S(1)} collective-permute-done((bf16[8,64,128]{2,1,0:T(8,128)(2,1)S(1)}, bf16[8,64,128]{2,1,0:T(8,128)(2,1)S(1)}, u32[]{:S(2)}, u32[]{:S(2)}) %collective-permute-start.13) | collective-permute-done | bytes 131104 | tf_op jit(solution)/shard_map/ppermute | solution.py:36
  65.4 3.8 %collective-permute-start.16 = (bf16[2,16,128]{2,1,0:T(8,128)(2,1)S(1)}, bf16[2,16,128]{2,1,0:T(8,128)(2,1)S(1)}, u32[]{:S(2)}, u32[]{:S(2)}) collective-permute-start(bf16[2,16,128]{2,1,0:T(8,128)(2,1)S(1)} %get-tuple-element.83), channel_id=1, source_target_pairs={{0,128},{4,132},{8,136},{12,140},{16,144},{20,148},{24,152},{28,15... | collective-permute-start | bytes 24584 | tf_op jit(solution)/shard_map/ppermute | solution.py:36
  73.4 3.2 %collective-permute-start.18 = (bf16[8,16,128]{2,1,0:T(8,128)(2,1)S(1)}, bf16[8,16,128]{2,1,0:T(8,128)(2,1)S(1)}, u32[]{:S(2)}, u32[]{:S(2)}) collective-permute-start(bf16[8,16,128]{2,1,0:T(8,128)(2,1)S(1)} %pad_maximum_fusion.10), channel_id=1, source_target_pairs={{0,4},{4,0},{8,12},{12,8},{16,20},{20,16},{24,28},{28,24},{32,36},... | collective-permute-start | bytes 98312 | tf_op jit(solution)/shard_map/ppermute | solution.py:36
  83.4 5.0 %collective-permute-start.19 = (bf16[16,16,128]{2,1,0:T(8,128)(2,1)S(1)}, bf16[16,16,128]{2,1,0:T(8,128)(2,1)S(1)}, u32[]{:S(2)}, u32[]{:S(2)}) collective-permute-start(bf16[16,16,128]{2,1,0:T(8,128)(2,1)S(1)} %constant_dynamic-update-slice_fusion), channel_id=1, source_target_pairs={{0,0},{4,36},{8,8},{12,44},{16,16},{20,52},{24,24},{28,60},{32,32}... | collective-permute-start | bytes 196616 | tf_op jit(solution)/shard_map/ppermute | solution.py:50
  89.9 3.1 %collective-permute-start.25 = (bf16[32,16,128]{2,1,0:T(8,128)(2,1)S(1)}, bf16[32,16,128]{2,1,0:T(8,128)(2,1)S(1)}, u32[]{:S(2)}, u32[]{:S(2)}) collective-permute-start(bf16[32,16,128]{2,1,0:T(8,128)(2,1)S(1)} %get-tuple-element.88), channel_id=1, source_target_pairs={{0,192},{4,196},{8,200},{12,204},{16,208},{20,212},{24,216},{28,22... | collective-permute-start | bytes 393224 | tf_op jit(solution)/shard_map/ppermute | solution.py:36
  103.5 3.7 %collective-permute-start.28 = (bf16[16,16,128]{2,1,0:T(8,128)(2,1)S(1)}, bf16[16,16,128]{2,1,0:T(8,128)(2,1)S(1)}, u32[]{:S(2)}, u32[]{:S(2)}) collective-permute-start(bf16[16,16,128]{2,1,0:T(8,128)(2,1)S(1)} %pad_maximum_fusion.5), channel_id=1, source_target_pairs={{0,0},{4,36},{8,8},{12,44},{16,16},{20,52},{24,24},{28,60},{32,32}... | collective-permute-start | bytes 196616 | tf_op jit(solution)/shard_map/ppermute | solution.py:50
  113.6 3.0 %collective-permute-done.29 = bf16[16,16,128]{2,1,0:T(8,128)(2,1)S(1)} collective-permute-done((bf16[16,16,128]{2,1,0:T(8,128)(2,1)S(1)}, bf16[16,16,128]{2,1,0:T(8,128)(2,1)S(1)}, u32[]{:S(2)}, u32[]{:S(2)}) %collective-permute-start.29) | collective-permute-done | bytes 65568 | tf_op jit(solution)/shard_map/ppermute | solution.py:50
  122.9 4.2 %collective-permute-start.34 = (bf16[16,16,128]{2,1,0:T(8,128)(2,1)S(1)}, bf16[16,16,128]{2,1,0:T(8,128)(2,1)S(1)}, u32[]{:S(2)}, u32[]{:S(2)}) collective-permute-start(bf16[16,16,128]{2,1,0:T(8,128)(2,1)S(1)} %pad_maximum_fusion.6), channel_id=1, source_target_pairs={{0,0},{4,36},{8,8},{12,44},{16,16},{20,52},{24,24},{28,60},{32,32}... | collective-permute-start | bytes 196616 | tf_op jit(solution)/shard_map/ppermute | solution.py:50
  127.1 5.0 %collective-permute-start.35 = (bf16[16,16,128]{2,1,0:T(8,128)(2,1)S(1)}, bf16[16,16,128]{2,1,0:T(8,128)(2,1)S(1)}, u32[]{:S(2)}, u32[]{:S(2)}) collective-permute-start(bf16[16,16,128]{2,1,0:T(8,128)(2,1)S(1)} %pad_maximum_fusion.6), channel_id=1, source_target_pairs={{0,8},{4,44},{8,0},{12,36},{16,24},{20,60},{24,16},{28,52},{32,40}... | collective-permute-start | bytes 196616 | tf_op jit(solution)/shard_map/ppermute | solution.py:50
  144.5 3.4 %collective-permute-start.42 = (bf16[16,16,128]{2,1,0:T(8,128)(2,1)S(1)}, bf16[16,16,128]{2,1,0:T(8,128)(2,1)S(1)}, u32[]{:S(2)}, u32[]{:S(2)}) collective-permute-start(bf16[16,16,128]{2,1,0:T(8,128)(2,1)S(1)} %pad_maximum_fusion.7), channel_id=1, source_target_pairs={{0,16},{4,52},{8,24},{12,60},{16,0},{20,36},{24,8},{28,44},{32,48}... | collective-permute-start | bytes 196616 | tf_op jit(solution)/shard_map/ppermute | solution.py:50
  148.6 5.8 %collective-permute-start.40 = (bf16[16,16,128]{2,1,0:T(8,128)(2,1)S(1)}, bf16[16,16,128]{2,1,0:T(8,128)(2,1)S(1)}, u32[]{:S(2)}, u32[]{:S(2)}) collective-permute-start(bf16[16,16,128]{2,1,0:T(8,128)(2,1)S(1)} %pad_maximum_fusion.7), channel_id=1, source_target_pairs={{0,0},{4,36},{8,8},{12,44},{16,16},{20,52},{24,24},{28,60},{32,32}... | collective-permute-start | bytes 196616 | tf_op jit(solution)/shard_map/ppermute | solution.py:50
  154.5 3.1 %collective-permute-done.40 = bf16[16,16,128]{2,1,0:T(8,128)(2,1)S(1)} collective-permute-done((bf16[16,16,128]{2,1,0:T(8,128)(2,1)S(1)}, bf16[16,16,128]{2,1,0:T(8,128)(2,1)S(1)}, u32[]{:S(2)}, u32[]{:S(2)}) %collective-permute-start.40) | collective-permute-done | bytes 65568 | tf_op jit(solution)/shard_map/ppermute | solution.py:50
  164.9 5.8 %collective-permute-start.46 = (bf16[16,16,128]{2,1,0:T(8,128)(2,1)S(1)}, bf16[16,16,128]{2,1,0:T(8,128)(2,1)S(1)}, u32[]{:S(2)}, u32[]{:S(2)}) collective-permute-start(bf16[16,16,128]{2,1,0:T(8,128)(2,1)S(1)} %pad_maximum_fusion.8), channel_id=1, source_target_pairs={{0,0},{4,36},{8,8},{12,44},{16,16},{20,52},{24,24},{28,60},{32,32}... | collective-permute-start | bytes 196616 | tf_op jit(solution)/shard_map/ppermute | solution.py:50
  170.8 4.1 %collective-permute-start.47 = (bf16[16,16,128]{2,1,0:T(8,128)(2,1)S(1)}, bf16[16,16,128]{2,1,0:T(8,128)(2,1)S(1)}, u32[]{:S(2)}, u32[]{:S(2)}) collective-permute-start(bf16[16,16,128]{2,1,0:T(8,128)(2,1)S(1)} %pad_maximum_fusion.8), channel_id=1, source_target_pairs={{0,8},{4,44},{8,0},{12,36},{16,24},{20,60},{24,16},{28,52},{32,40}... | collective-permute-start | bytes 196616 | tf_op jit(solution)/shard_map/ppermute | solution.py:50
  175.0 3.0 %collective-permute-done.47 = bf16[16,16,128]{2,1,0:T(8,128)(2,1)S(1)} collective-permute-done((bf16[16,16,128]{2,1,0:T(8,128)(2,1)S(1)}, bf16[16,16,128]{2,1,0:T(8,128)(2,1)S(1)}, u32[]{:S(2)}, u32[]{:S(2)}) %collective-permute-start.47) | collective-permute-done | bytes 65568 | tf_op jit(solution)/shard_map/ppermute | solution.py:50
  185.2 4.8 %collective-permute-start.52 = (bf16[16,16,128]{2,1,0:T(8,128)(2,1)S(1)}, bf16[16,16,128]{2,1,0:T(8,128)(2,1)S(1)}, u32[]{:S(2)}, u32[]{:S(2)}) collective-permute-start(bf16[16,16,128]{2,1,0:T(8,128)(2,1)S(1)} %pad_maximum_fusion.9), channel_id=1, source_target_pairs={{0,0},{4,36},{8,8},{12,44},{16,16},{20,52},{24,24},{28,60},{32,32}... | collective-permute-start | bytes 196616 | tf_op jit(solution)/shard_map/ppermute | solution.py:50
  190.1 3.2 %collective-permute-start.53 = (bf16[16,16,128]{2,1,0:T(8,128)(2,1)S(1)}, bf16[16,16,128]{2,1,0:T(8,128)(2,1)S(1)}, u32[]{:S(2)}, u32[]{:S(2)}) collective-permute-start(bf16[16,16,128]{2,1,0:T(8,128)(2,1)S(1)} %pad_maximum_fusion.9), channel_id=1, source_target_pairs={{0,8},{4,44},{8,0},{12,36},{16,24},{20,60},{24,16},{28,52},{32,40}... | collective-permute-start | bytes 196616 | tf_op jit(solution)/shard_map/ppermute | solution.py:50
  204.2 4.8 %collective-permute-start.58 = (bf16[12,16,128]{2,1,0:T(8,128)(2,1)S(1)}, bf16[12,16,128]{2,1,0:T(8,128)(2,1)S(1)}, u32[]{:S(2)}, u32[]{:S(2)}) collective-permute-start(bf16[12,16,128]{2,1,0:T(8,128)(2,1)S(1)} %get-tuple-element.101), channel_id=1, source_target_pairs={{0,128},{4,132},{8,136},{12,140},{16,144},{20,148},{24,152},{28,15... | collective-permute-start | bytes 147464 | tf_op jit(solution)/shard_map/ppermute | solution.py:36
  (202 shorter events, 113.9 us)
Async XLA Ops:
  6.5 89.9 %all-gather.5.cloned.1.call-start = ((), (), s32[]{:S(2)}) async-start(), calls=%async_computation | async-start | bytes 4456448 | tf_op jit(solution)/shard_map/all_gather | solution.py:261
  11.5 146.1 %all-gather.7.cloned.1.call-start = ((), (), s32[]{:S(2)}) async-start(), calls=%async_computation.1 | async-start | bytes 4456448 | tf_op jit(solution)/shard_map/all_gather | solution.py:261
  19.0 11.5 %collective-permute-start.7 = (bf16[2,128,128]{2,1,0:T(8,128)(2,1)}, bf16[2,128,128]{2,1,0:T(8,128)(2,1)S(1)}, u32[]{:S(2)}, u32[]{:S(2)}) collective-permute-start(bf16[2,128,128]{2,1,0:T(8,128)(2,1)} %get-tuple-element.58), channel_id=1, source_target_pairs={{0,3},{1,2},{2,1},{3,0},{4,7},{5,6},{6,5},{7,4},{8,11},{9,10},{10,... | collective-permute-start | bytes 196616 | tf_op jit(solution)/shard_map/ppermute | solution.py:272
  19.8 14.3 %collective-permute-start.6 = (bf16[2,128,128]{2,1,0:T(8,128)(2,1)}, bf16[2,128,128]{2,1,0:T(8,128)(2,1)S(1)}, u32[]{:S(2)}, u32[]{:S(2)}) collective-permute-start(bf16[2,128,128]{2,1,0:T(8,128)(2,1)} %get-tuple-element.58), channel_id=1, source_target_pairs={{0,2},{1,3},{2,0},{3,1},{4,6},{5,7},{6,4},{7,5},{8,10},{9,11},{10,... | collective-permute-start | bytes 196616 | tf_op jit(solution)/shard_map/ppermute | solution.py:272
  20.3 17.5 %collective-permute-start.5 = (bf16[2,128,128]{2,1,0:T(8,128)(2,1)}, bf16[2,128,128]{2,1,0:T(8,128)(2,1)S(1)}, u32[]{:S(2)}, u32[]{:S(2)}) collective-permute-start(bf16[2,128,128]{2,1,0:T(8,128)(2,1)} %get-tuple-element.58), channel_id=1, source_target_pairs={{0,1},{1,0},{2,3},{3,2},{4,5},{5,4},{6,7},{7,6},{8,9},{9,8},{10,11... | collective-permute-start | bytes 196616 | tf_op jit(solution)/shard_map/ppermute | solution.py:272
  22.4 17.7 %collective-permute-start.4 = (bf16[4,64,128]{2,1,0:T(8,128)(2,1)S(1)}, bf16[4,64,128]{2,1,0:T(8,128)(2,1)S(1)}, u32[]{:S(2)}, u32[]{:S(2)}) collective-permute-start(bf16[4,64,128]{2,1,0:T(8,128)(2,1)S(1)} %pad_maximum_fusion.4), channel_id=1, source_target_pairs={{0,24},{4,60},{8,16},{12,52},{16,8},{20,44},{24,0},{28,36},{32,56}... | collective-permute-start | bytes 196616 | tf_op jit(solution)/shard_map/ppermute | solution.py:50
  26.2 16.6 %collective-permute-start.3 = (bf16[4,64,128]{2,1,0:T(8,128)(2,1)S(1)}, bf16[4,64,128]{2,1,0:T(8,128)(2,1)S(1)}, u32[]{:S(2)}, u32[]{:S(2)}) collective-permute-start(bf16[4,64,128]{2,1,0:T(8,128)(2,1)S(1)} %pad_maximum_fusion.4), channel_id=1, source_target_pairs={{0,16},{4,52},{8,24},{12,60},{16,0},{20,36},{24,8},{28,44},{32,48}... | collective-permute-start | bytes 196616 | tf_op jit(solution)/shard_map/ppermute | solution.py:50
  30.5 12.3 %collective-permute-start.2 = (bf16[4,64,128]{2,1,0:T(8,128)(2,1)S(1)}, bf16[4,64,128]{2,1,0:T(8,128)(2,1)S(1)}, u32[]{:S(2)}, u32[]{:S(2)}) collective-permute-start(bf16[4,64,128]{2,1,0:T(8,128)(2,1)S(1)} %pad_maximum_fusion.4), channel_id=1, source_target_pairs={{0,8},{4,44},{8,0},{12,36},{16,24},{20,60},{24,16},{28,52},{32,40}... | collective-permute-start | bytes 196616 | tf_op jit(solution)/shard_map/ppermute | solution.py:50
  34.1 9.6 %collective-permute-start.1 = (bf16[4,64,128]{2,1,0:T(8,128)(2,1)S(1)}, bf16[4,64,128]{2,1,0:T(8,128)(2,1)S(1)}, u32[]{:S(2)}, u32[]{:S(2)}) collective-permute-start(bf16[4,64,128]{2,1,0:T(8,128)(2,1)S(1)} %pad_maximum_fusion.4), channel_id=1, source_target_pairs={{0,0},{4,36},{8,8},{12,44},{16,16},{20,52},{24,24},{28,60},{32,32}... | collective-permute-start | bytes 196616 | tf_op jit(solution)/shard_map/ppermute | solution.py:50
  51.2 10.8 %collective-permute-start.13 = (bf16[8,64,128]{2,1,0:T(8,128)(2,1)S(1)}, bf16[8,64,128]{2,1,0:T(8,128)(2,1)S(1)}, u32[]{:S(2)}, u32[]{:S(2)}) collective-permute-start(bf16[8,64,128]{2,1,0:T(8,128)(2,1)S(1)} %get-tuple-element.78), channel_id=1, source_target_pairs={{0,128},{4,132},{8,136},{12,140},{16,144},{20,148},{24,152},{28,15... | collective-permute-start | bytes 393224 | tf_op jit(solution)/shard_map/ppermute | solution.py:36
  52.5 11.8 %collective-permute-start.14 = (bf16[8,64,128]{2,1,0:T(8,128)(2,1)S(1)}, bf16[8,64,128]{2,1,0:T(8,128)(2,1)S(1)}, u32[]{:S(2)}, u32[]{:S(2)}) collective-permute-start(bf16[8,64,128]{2,1,0:T(8,128)(2,1)S(1)} %get-tuple-element.79), channel_id=1, source_target_pairs={{0,192},{4,196},{8,200},{12,204},{16,208},{20,212},{24,216},{28,22... | collective-permute-start | bytes 393224 | tf_op jit(solution)/shard_map/ppermute | solution.py:36
  77.5 11.6 %collective-permute-start.22 = (bf16[16,16,128]{2,1,0:T(8,128)(2,1)S(1)}, bf16[16,16,128]{2,1,0:T(8,128)(2,1)S(1)}, u32[]{:S(2)}, u32[]{:S(2)}) collective-permute-start(bf16[16,16,128]{2,1,0:T(8,128)(2,1)S(1)} %constant_dynamic-update-slice_fusion), channel_id=1, source_target_pairs={{0,24},{4,60},{8,16},{12,52},{16,8},{20,44},{24,0},{28,36},{32,56}... | collective-permute-start | bytes 196616 | tf_op jit(solution)/shard_map/ppermute | solution.py:50
  79.7 10.2 %collective-permute-start.21 = (bf16[16,16,128]{2,1,0:T(8,128)(2,1)S(1)}, bf16[16,16,128]{2,1,0:T(8,128)(2,1)S(1)}, u32[]{:S(2)}, u32[]{:S(2)}) collective-permute-start(bf16[16,16,128]{2,1,0:T(8,128)(2,1)S(1)} %constant_dynamic-update-slice_fusion), channel_id=1, source_target_pairs={{0,16},{4,52},{8,24},{12,60},{16,0},{20,36},{24,8},{28,44},{32,48}... | collective-permute-start | bytes 196616 | tf_op jit(solution)/shard_map/ppermute | solution.py:50
  81.2 11.8 %collective-permute-start.20 = (bf16[16,16,128]{2,1,0:T(8,128)(2,1)S(1)}, bf16[16,16,128]{2,1,0:T(8,128)(2,1)S(1)}, u32[]{:S(2)}, u32[]{:S(2)}) collective-permute-start(bf16[16,16,128]{2,1,0:T(8,128)(2,1)S(1)} %constant_dynamic-update-slice_fusion), channel_id=1, source_target_pairs={{0,8},{4,44},{8,0},{12,36},{16,24},{20,60},{24,16},{28,52},{32,40}... | collective-permute-start | bytes 196616 | tf_op jit(solution)/shard_map/ppermute | solution.py:50
  83.4 9.5 %collective-permute-start.19 = (bf16[16,16,128]{2,1,0:T(8,128)(2,1)S(1)}, bf16[16,16,128]{2,1,0:T(8,128)(2,1)S(1)}, u32[]{:S(2)}, u32[]{:S(2)}) collective-permute-start(bf16[16,16,128]{2,1,0:T(8,128)(2,1)S(1)} %constant_dynamic-update-slice_fusion), channel_id=1, source_target_pairs={{0,0},{4,36},{8,8},{12,44},{16,16},{20,52},{24,24},{28,60},{32,32}... | collective-permute-start | bytes 196616 | tf_op jit(solution)/shard_map/ppermute | solution.py:50
  103.5 10.1 %collective-permute-start.28 = (bf16[16,16,128]{2,1,0:T(8,128)(2,1)S(1)}, bf16[16,16,128]{2,1,0:T(8,128)(2,1)S(1)}, u32[]{:S(2)}, u32[]{:S(2)}) collective-permute-start(bf16[16,16,128]{2,1,0:T(8,128)(2,1)S(1)} %pad_maximum_fusion.5), channel_id=1, source_target_pairs={{0,0},{4,36},{8,8},{12,44},{16,16},{20,52},{24,24},{28,60},{32,32}... | collective-permute-start | bytes 196616 | tf_op jit(solution)/shard_map/ppermute | solution.py:50
  107.3 9.4 %collective-permute-start.29 = (bf16[16,16,128]{2,1,0:T(8,128)(2,1)S(1)}, bf16[16,16,128]{2,1,0:T(8,128)(2,1)S(1)}, u32[]{:S(2)}, u32[]{:S(2)}) collective-permute-start(bf16[16,16,128]{2,1,0:T(8,128)(2,1)S(1)} %pad_maximum_fusion.5), channel_id=1, source_target_pairs={{0,8},{4,44},{8,0},{12,36},{16,24},{20,60},{24,16},{28,52},{32,40}... | collective-permute-start | bytes 196616 | tf_op jit(solution)/shard_map/ppermute | solution.py:50
  122.9 10.1 %collective-permute-start.34 = (bf16[16,16,128]{2,1,0:T(8,128)(2,1)S(1)}, bf16[16,16,128]{2,1,0:T(8,128)(2,1)S(1)}, u32[]{:S(2)}, u32[]{:S(2)}) collective-permute-start(bf16[16,16,128]{2,1,0:T(8,128)(2,1)S(1)} %pad_maximum_fusion.6), channel_id=1, source_target_pairs={{0,0},{4,36},{8,8},{12,44},{16,16},{20,52},{24,24},{28,60},{32,32}... | collective-permute-start | bytes 196616 | tf_op jit(solution)/shard_map/ppermute | solution.py:50
  127.1 7.9 %collective-permute-start.35 = (bf16[16,16,128]{2,1,0:T(8,128)(2,1)S(1)}, bf16[16,16,128]{2,1,0:T(8,128)(2,1)S(1)}, u32[]{:S(2)}, u32[]{:S(2)}) collective-permute-start(bf16[16,16,128]{2,1,0:T(8,128)(2,1)S(1)} %pad_maximum_fusion.6), channel_id=1, source_target_pairs={{0,8},{4,44},{8,0},{12,36},{16,24},{20,60},{24,16},{28,52},{32,40}... | collective-permute-start | bytes 196616 | tf_op jit(solution)/shard_map/ppermute | solution.py:50
  142.6 11.8 %collective-permute-start.43 = (bf16[16,16,128]{2,1,0:T(8,128)(2,1)S(1)}, bf16[16,16,128]{2,1,0:T(8,128)(2,1)S(1)}, u32[]{:S(2)}, u32[]{:S(2)}) collective-permute-start(bf16[16,16,128]{2,1,0:T(8,128)(2,1)S(1)} %pad_maximum_fusion.7), channel_id=1, source_target_pairs={{0,24},{4,60},{8,16},{12,52},{16,8},{20,44},{24,0},{28,36},{32,56}... | collective-permute-start | bytes 196616 | tf_op jit(solution)/shard_map/ppermute | solution.py:50
  144.5 10.0 %collective-permute-start.42 = (bf16[16,16,128]{2,1,0:T(8,128)(2,1)S(1)}, bf16[16,16,128]{2,1,0:T(8,128)(2,1)S(1)}, u32[]{:S(2)}, u32[]{:S(2)}) collective-permute-start(bf16[16,16,128]{2,1,0:T(8,128)(2,1)S(1)} %pad_maximum_fusion.7), channel_id=1, source_target_pairs={{0,16},{4,52},{8,24},{12,60},{16,0},{20,36},{24,8},{28,44},{32,48}... | collective-permute-start | bytes 196616 | tf_op jit(solution)/shard_map/ppermute | solution.py:50
  148.6 8.9 %collective-permute-start.40 = (bf16[16,16,128]{2,1,0:T(8,128)(2,1)S(1)}, bf16[16,16,128]{2,1,0:T(8,128)(2,1)S(1)}, u32[]{:S(2)}, u32[]{:S(2)}) collective-permute-start(bf16[16,16,128]{2,1,0:T(8,128)(2,1)S(1)} %pad_maximum_fusion.7), channel_id=1, source_target_pairs={{0,0},{4,36},{8,8},{12,44},{16,16},{20,52},{24,24},{28,60},{32,32}... | collective-permute-start | bytes 196616 | tf_op jit(solution)/shard_map/ppermute | solution.py:50
  164.9 10.1 %collective-permute-start.46 = (bf16[16,16,128]{2,1,0:T(8,128)(2,1)S(1)}, bf16[16,16,128]{2,1,0:T(8,128)(2,1)S(1)}, u32[]{:S(2)}, u32[]{:S(2)}) collective-permute-start(bf16[16,16,128]{2,1,0:T(8,128)(2,1)S(1)} %pad_maximum_fusion.8), channel_id=1, source_target_pairs={{0,0},{4,36},{8,8},{12,44},{16,16},{20,52},{24,24},{28,60},{32,32}... | collective-permute-start | bytes 196616 | tf_op jit(solution)/shard_map/ppermute | solution.py:50
  185.2 10.9 %collective-permute-start.52 = (bf16[16,16,128]{2,1,0:T(8,128)(2,1)S(1)}, bf16[16,16,128]{2,1,0:T(8,128)(2,1)S(1)}, u32[]{:S(2)}, u32[]{:S(2)}) collective-permute-start(bf16[16,16,128]{2,1,0:T(8,128)(2,1)S(1)} %pad_maximum_fusion.9), channel_id=1, source_target_pairs={{0,0},{4,36},{8,8},{12,44},{16,16},{20,52},{24,24},{28,60},{32,32}... | collective-permute-start | bytes 196616 | tf_op jit(solution)/shard_map/ppermute | solution.py:50
  (47 other events, 261.8 us)
Sparse Core Ops, SparseCore 0:
  11.6 66.7 all-gather.4
  80.8 55.3 all-gather.6
